TPU v7x, 32 devices: a whole 2x2x4 slice. The times are simulated.
32 devices in a mesh: batch: 4 (over y, core), blk: 8 (over z, x).
Axes of the slice: x: 2, y: 2, z: 4, core: 2. Of those that a mesh axis runs over, the one named last changes fastest.
Arguments:
- inputs: bfloat16 [12, 2048, 1024], P('batch', 'blk'), may hold values from -6 to 6
- ln_attn: float32 [1024], replicated, may hold values from 0.1 to 1.9
- w_query: bfloat16 [1024, 1024], replicated, may hold values from -0.1875 to 0.1875
- w_key: bfloat16 [1024, 1024], replicated, may hold values from -0.1875 to 0.1875
- w_value: bfloat16 [1024, 1024], replicated, may hold values from -0.1875 to 0.1875
- w_out: bfloat16 [1024, 1024], replicated, may hold values from -0.1875 to 0.1875
- head_scale: float32 [16], replicated, may hold values from 0.5 to 2
- ln_post: float32 [1024], replicated, may hold values from 0.1 to 1.9
- ln_ffn: float32 [1024], replicated, may hold values from 0.1 to 1.9
- w_fc1: bfloat16 [1024, 4096], replicated, may hold values from -0.1875 to 0.1875
- ln_mid: float32 [4096], replicated, may hold values from 0.1 to 1.9
- w_fc2: bfloat16 [4096, 1024], replicated, may hold values from -0.09375 to 0.09375
- offsets: int32 [12, 4], P('batch'), may hold values from 0 to 2047, as said below
- cotangent: bfloat16 [12, 2048, 1024], P('batch', 'blk'), may hold values from -6 to 6
Outputs:
- layer_out: bfloat16 [12, 2048, 1024], P('batch', 'blk')
- grad_inputs: float32 [12, 2048, 1024], P('batch', 'blk')
- grad_ln_attn: float32 [1024], P('blk')
- grad_w_query: float32 [1024, 1024], P('blk')
- grad_w_key: float32 [1024, 1024], P('blk')
- grad_w_value: float32 [1024, 1024], P('blk')
- grad_w_out: float32 [1024, 1024], P('blk')
- grad_head_scale: float32 [16], replicated
- grad_ln_post: float32 [1024], P('blk')
- grad_ln_ffn: float32 [1024], P('blk')
- grad_w_fc1: float32 [1024, 4096], P('blk')
- grad_ln_mid: float32 [4096], P('blk')
- grad_w_fc2: float32 [4096, 1024], P('blk')
Inputs may be any that keep to these rules, and one draw needn't show every extreme that they name: In each row offsets rise strictly from offsets[r, 0] = 0. In each aligned block of 3 rows one row has a document that begins within its first 256 positions and ends within its last 256, and its last document is a single position.
All inputs are finite; a program needn't handle non-finite values.
Results may differ from a plain program's by a relative error of at most 0.02.
Values may be sent and summed in bfloat16 or wider, within the bound.
No kernel may reach another device: no remote copies, remote signals or barrier semaphores. Data moves between devices by JAX's collectives and lax.ppermute only.
A program may use at most 256 MiB of HBM per device.

v0:
```python
import functools

import jax
import jax.numpy as jnp
from jax import lax
from jax.experimental import pallas as pl
from jax.experimental.pallas import tpu as pltpu
from jax.sharding import PartitionSpec as P

EPSILON = 1e-05
MASKED = -1e30
VMEM_BYTES = 50 * 1024 * 1024
F32 = jnp.float32
BF16 = jnp.bfloat16
LAST = (((1,), (1,)), ((), ()))
FIRST = (((0,), (0,)), ((), ()))
SMEM = pl.BlockSpec(memory_space=pltpu.SMEM)
VMEM = pl.BlockSpec(memory_space=pltpu.VMEM)


def dot_last(left, right):
    return lax.dot_general(left, right, LAST, preferred_element_type=F32)


def dot_first(left, right):
    return lax.dot_general(left, right, FIRST, preferred_element_type=F32)


def dot(left, right):
    return jnp.dot(left, right, preferred_element_type=F32)


def kernel_params():
    return pltpu.CompilerParams(vmem_limit_bytes=VMEM_BYTES)


def cost(flops, size):
    return pl.CostEstimate(flops=int(flops), bytes_accessed=int(size), transcendentals=0)


def exchange(parts):
    return lax.all_to_all(parts, "blk", 0, 0, tiled=True)


def norm_parts(rows_in):
    average = jnp.mean(rows_in, axis=-1, keepdims=True)
    centred = rows_in - average
    spread = lax.rsqrt(jnp.mean(centred * centred, axis=-1, keepdims=True) + EPSILON)
    return centred * spread, spread


def norm_back(hat, spread, gain, grad):
    weighted = grad * gain
    return spread * (
        weighted
        - jnp.mean(weighted, axis=-1, keepdims=True)
        - hat * jnp.mean(weighted * hat, axis=-1, keepdims=True)
    )


def rows_by_work(offs_ref, length):
    rows, docs = offs_ref.shape
    work = []
    for r in range(rows):
        total = jnp.int32(0)
        for d in range(docs):
            end = offs_ref[r, d + 1] if d + 1 < docs else length
            total += (end - offs_ref[r, d]) * (end - offs_ref[r, d])
        work.append(total)
    ranks = []
    for r in range(rows):
        rank = jnp.int32(0)
        for other in range(rows):
            if other < r:
                rank += (work[other] >= work[r]).astype(jnp.int32)
            elif other > r:
                rank += (work[other] > work[r]).astype(jnp.int32)
        ranks.append(rank)
    return [
        sum(jnp.where(ranks[r] == slot, jnp.int32(r), jnp.int32(0)) for r in range(rows))
        for slot in range(rows)
    ]


def project_kernel(
    slot,
    offs_ref,
    gain_ref,
    x_hbm,
    wq_hbm,
    wk_hbm,
    wv_hbm,
    normed_ref,
    out_ref,
    order_ref,
    x_ref,
    weight_ref,
    sems,
):
    group, _, span, width = out_ref.shape
    order = rows_by_work(offs_ref, group * span)
    copy_x = pltpu.make_async_copy(x_hbm.at[order[slot]], x_ref, sems.at[3])
    copy_x.start()
    copies = [
        pltpu.make_async_copy(weight, weight_ref.at[n], sems.at[n])
        for n, weight in enumerate((wq_hbm, wk_hbm, wv_hbm))
    ]
    for copy in copies:
        copy.start()
    for r, row in enumerate(order):
        order_ref[r] = row
    copy_x.wait()
    hat, _ = norm_parts(x_ref[...].astype(F32))
    normed = (hat * gain_ref[...]).astype(BF16)
    normed_ref[...] = normed
    for n in range(3):
        copies[n].wait()
        product = dot(normed, weight_ref[n]).astype(BF16)
        for s in range(group):
            out_ref[s, n] = product[:, s * width : (s + 1) * width]


def project(offsets, slot, x, gain, w_query, w_key, w_value, group):
    rows, span, model = x.shape
    return pl.pallas_call(
        functools.partial(project_kernel, slot),
        in_specs=[SMEM, VMEM] + [pl.BlockSpec(memory_space=pl.ANY)] * 4,
        out_specs=[VMEM, VMEM, SMEM],
        scratch_shapes=[
            pltpu.VMEM((span, model), BF16),
            pltpu.VMEM((3, model, model), BF16),
            pltpu.SemaphoreType.DMA((4,)),
        ],
        out_shape=[
            jax.ShapeDtypeStruct((span, model), BF16),
            jax.ShapeDtypeStruct((group, 3, span, model // group), BF16),
            jax.ShapeDtypeStruct((rows,), jnp.int32),
        ],
        compiler_params=kernel_params(),
        cost_estimate=cost(0, 1024),
        name="project",
    )(offsets, gain, x, w_query, w_key, w_value)


def doc_start(offs_ref, row, pos):
    start = jnp.zeros_like(pos)
    for d in range(offs_ref.shape[1]):
        first = offs_ref[row, d]
        start = jnp.where(pos >= first, first, start)
    return start


def doc_end(offs_ref, row, pos, length):
    end = jnp.int32(length)
    for d in reversed(range(offs_ref.shape[1])):
        first = offs_ref[row, d]
        end = jnp.where(first > pos, first, end)
    return end


def head_lanes(shape, head, head_dim):
    lane = lax.broadcasted_iota(jnp.int32, shape, 1)
    return (lane >= head * head_dim) & (lane < (head + 1) * head_dim)


def attend_kernel(slot, heads, head_dim, order_ref, offs_ref, scale_ref, held, *refs):
    result_ref, lse_ref, score_ref = refs[-3:]
    attend_row(
        order_ref[slot], heads, head_dim, offs_ref, scale_ref, held, result_ref, lse_ref, score_ref
    )


def attend_row(
    row, heads, head_dim, offs_ref, scale_ref, held, result_ref, lse_ref, score_ref
):
    blocks, _, span, width = held.shape
    wide = score_ref.shape[-1]
    per = wide // span
    lanes = min(128, wide)
    score_scale = head_dim ** (-0.5)

    def query_block(i, carry):
        first_pos = i * span
        queries = held[i, 0] * jnp.asarray(score_scale, BF16)
        query_head = [
            jnp.where(head_lanes((span, width), h, head_dim), queries, 0).astype(BF16)
            for h in range(heads)
        ]
        query_pos = first_pos + lax.broadcasted_iota(jnp.int32, (span, 1), 0)
        query_start = doc_start(offs_ref, row, query_pos)
        low = doc_start(offs_ref, row, first_pos) // wide
        high = (first_pos + span - 1) // wide + 1

        def score_step(j, tops):
            keys = held[pl.ds(j * per, per), 1].reshape(wide, width)
            key_pos = j * wide + lax.broadcasted_iota(jnp.int32, (span, wide), 1)
            allowed = (key_pos >= query_start) & (key_pos <= query_pos)
            new = []
            for h in range(heads):
                scores = jnp.where(allowed, dot_last(query_head[h], keys), MASKED)
                score_ref[h, j] = scores
                top = tops[h]
                for c in range(0, wide, lanes):
                    top = jnp.maximum(top, scores[:, c : c + lanes])
                new.append(top)
            return tuple(new)

        tops = lax.fori_loop(
            low, high, score_step, tuple(jnp.full((span, lanes), MASKED, F32) for h in range(heads))
        )
        tops = [jnp.max(top, axis=1, keepdims=True) for top in tops]

        def value_step(j, state):
            values = held[pl.ds(j * per, per), 2].reshape(wide, width)
            new = []
            for h in range(heads):
                total, acc = state[h]
                probs = jnp.exp(score_ref[h, j] - tops[h])
                for c in range(0, wide, lanes):
                    total = total + probs[:, c : c + lanes]
                acc = acc + dot(probs.astype(BF16), values)
                new.append((total, acc))
            return tuple(new)

        state = lax.fori_loop(
            low,
            high,
            value_step,
            tuple(
                (jnp.zeros((span, lanes), F32), jnp.zeros((span, width), F32)) for h in range(heads)
            ),
        )
        result = jnp.zeros((span, width), F32)
        for h in range(heads):
            total = jnp.sum(state[h][0], axis=1, keepdims=True)
            result = jnp.where(head_lanes((span, width), h, head_dim), state[h][1] / total, result)
            log_total = tops[h] + jnp.log(total)
            lse_ref[i, h : h + 1, :] = jnp.transpose(jnp.broadcast_to(log_total, (span, 128)))[
                0:1, :
            ]
        result_ref[i] = (result * scale_ref[...]).astype(BF16)
        return carry

    lax.fori_loop(0, blocks, query_block, 0)


def attend(order, offsets, slot, qkv, scale_lanes, heads, head_dim, at=0, count=1, into=None):
    group, _, span, width = qkv.shape
    length = group * span
    wide = max(span, min(512, length))
    held = [] if into is None else [into]
    return pl.pallas_call(
        functools.partial(attend_kernel, slot, heads, head_dim),
        grid=(1,),
        in_specs=[SMEM, SMEM, VMEM, VMEM] + [pl.BlockSpec(memory_space=pl.ANY)] * len(held),
        out_specs=[pl.BlockSpec((group, None, span, width), lambda i: (0, at, 0, 0)), VMEM],
        out_shape=[
            jax.ShapeDtypeStruct((group, count, span, width), BF16),
            jax.ShapeDtypeStruct((group, heads, span), F32),
        ],
        scratch_shapes=[pltpu.VMEM((heads, length // wide, span, wide), F32)],
        input_output_aliases={4: 0} if held else {},
        compiler_params=kernel_params(),
        cost_estimate=cost(0, 1024),
        name="attend",
    )(order, offsets, scale_lanes, qkv, *held)


def attend_back_kernel(slot, heads, head_dim, order_ref, offs_ref, *refs):
    attend_back_row(order_ref[slot], heads, head_dim, offs_ref, *refs)


def attend_back_row(
    row,
    heads,
    head_dim,
    offs_ref,
    inv_ref,
    lse_ref,
    held,
    grad_ref,
    out_ref,
    dqkv_ref,
    total_ref,
    q_ref,
    k_ref,
    g_ref,
    delta_ref,
    dq_ref,
):
    blocks, _, span, width = held.shape
    score_scale = head_dim ** (-0.5)
    picks = lax.broadcasted_iota(jnp.int32, (8, width), 0)
    lane = lax.broadcasted_iota(jnp.int32, (8, width), 1)
    ones = jnp.where(lane // head_dim == picks, 1.0, 0.0).astype(F32)

    def prepare(i, carry):
        queries = held[i, 0] * jnp.asarray(score_scale, BF16)
        keys = held[i, 1]
        grads = grad_ref[i]
        for h in range(heads):
            mine = head_lanes((span, width), h, head_dim)
            q_ref[h, i] = jnp.where(mine, queries, 0).astype(BF16)
            k_ref[h, i] = jnp.where(mine, keys, 0).astype(BF16)
            g_ref[h, i] = jnp.where(mine, grads, 0).astype(BF16)
        product = grads.astype(F32) * out_ref[i].astype(F32) * inv_ref[...]
        delta_ref[i] = lax.dot_general(
            ones, product, LAST, precision=lax.Precision.HIGHEST, preferred_element_type=F32
        )
        dq_ref[i] = jnp.zeros((span, width), F32)
        return carry + delta_ref[i]

    per = 2 if span * 2 <= 512 and blocks % 2 == 0 else 1
    wide = per * span
    total_ref[...] = lax.fori_loop(0, blocks, prepare, jnp.zeros((8, span), F32))

    def key_block(j, carry):
        keys = held[j, 1]
        values = held[j, 2]
        key_pos = j * span + lax.broadcasted_iota(jnp.int32, (span, 1), 0)
        last = (doc_end(offs_ref, row, (j + 1) * span - 1, blocks * span) - 1) // wide + 1

        def query_step(i, state):
            dk, dv = state
            query_pos = i * wide + lax.broadcasted_iota(jnp.int32, (1, wide), 1)
            query_start = doc_start(offs_ref, row, query_pos)
            allowed = (key_pos >= query_start) & (key_pos <= query_pos)
            at = pl.ds(i * per, per)
            dq = dq_ref[at].reshape(wide, width)
            for h in range(heads):
                queries = q_ref[h, at].reshape(wide, width)
                grads = g_ref[h, at].reshape(wide, width)
                log_total = jnp.concatenate(
                    [lse_ref[i * per + n, h : h + 1, :] for n in range(per)], axis=1
                )
                delta = jnp.concatenate(
                    [delta_ref[i * per + n, h : h + 1, :] for n in range(per)], axis=1
                )
                scores = dot_last(keys, queries)
                probs = jnp.exp(jnp.where(allowed, scores - log_total, MASKED))
                d_scores = (probs * (dot_last(values, grads) - delta)).astype(BF16)
                dv = dv + dot(probs.astype(BF16), grads)
                dk = dk + dot(d_scores, queries)
                dq = dq + dot_first(d_scores, k_ref[h, j])
            dq_ref[at] = dq.reshape(per, span, width)
            return (dk, dv)

        zero = jnp.zeros((span, width), F32)
        dk, dv = lax.fori_loop(j // per, last, query_step, (zero, zero))
        dqkv_ref[j, 1] = dk.astype(BF16)
        dqkv_ref[j, 2] = dv.astype(BF16)
        dqkv_ref[j, 0] = (dq_ref[j] * score_scale).astype(BF16)
        return carry

    lax.fori_loop(0, blocks, key_block, 0)


def attend_back(
    order, offsets, slot, qkv, grads, grads_at, scaled, scaled_at, inverse_lanes, lse, heads, head_dim
):
    group, _, span, width = qkv.shape

    def block_spec(at):
        return pl.BlockSpec((group, None, span, width), lambda i: (0, at, 0, 0))

    return pl.pallas_call(
        functools.partial(attend_back_kernel, slot, heads, head_dim),
        grid=(1,),
        in_specs=[SMEM, SMEM, VMEM, VMEM, VMEM, block_spec(grads_at), block_spec(scaled_at)],
        out_specs=[pl.BlockSpec((group, None, 3, span, width), lambda i: (0, 0, 0, 0, 0)), VMEM],
        out_shape=[
            jax.ShapeDtypeStruct((group, 1, 3, span, width), BF16),
            jax.ShapeDtypeStruct((8, span), F32),
        ],
        scratch_shapes=[pltpu.VMEM((heads, group, span, width), BF16)] * 3
        + [pltpu.VMEM((group, 8, span), F32), pltpu.VMEM((group, span, width), F32)],
        compiler_params=kernel_params(),
        cost_estimate=cost(0, 1024),
        name="attend_back",
    )(order, offsets, inverse_lanes, lse, qkv, grads, scaled)


def join_grads_kernel(parts, in_ref, out_ref, value_ref):
    group = in_ref.shape[0]
    for n in range(3):
        whole = jnp.concatenate([in_ref[s, 0, n] for s in range(group)], axis=1)
        piece = whole.shape[1] // parts
        if n == 2:
            value_ref[...] = whole
            continue
        for p in range(parts):
            to = (p * 2 + n) * piece
            out_ref[:, to : to + piece] = whole[:, p * piece : (p + 1) * piece]


def join_grads(block):
    group, _, _, span, width = block.shape
    return pl.pallas_call(
        functools.partial(join_grads_kernel, PARTS),
        out_shape=[
            jax.ShapeDtypeStruct((span, 2 * group * width), BF16),
            jax.ShapeDtypeStruct((span, group * width), BF16),
        ],
        compiler_params=kernel_params(),
        cost_estimate=cost(0, 1024),
        name="join_grads",
    )(block)


FF_STEP = 1024
LAYER_VMEM = 62 * 1024 * 1024


def layer_kernel(
    slots,
    order_ref,
    post_ref,
    ffn_ref,
    mid_gain_ref,
    scale_ref,
    w_out_ref,
    x_hbm,
    d_out_hbm,
    d_mid_hbm,
    w_fc1_hbm,
    *refs,
):
    count = len(slots)
    o_refs = refs[:count]
    (
        scaled_ref,
        ffn_in_ref,
        residual_ref,
        mid_ref,
        d_pre_ref,
        d_proj_ref,
        d_residual_ref,
        d_attn_ref,
        g_post_ref,
        g_ffn_ref,
        g_mid_ref,
        x_ref,
        d_out_ref,
        d_mid_ref,
        w_fc1_ref,
        act_ref,
        slope_ref,
        sems,
        row_sems,
    ) = refs[count:]
    group, _, span, width = o_refs[0].shape
    tokens, hidden = act_ref.shape
    step = FF_STEP // count
    steps = [slice(c, c + step) for c in range(0, hidden, step)]
    weight_copies = [
        pltpu.make_async_copy(
            w_fc1_hbm.at[:, c : c + FF_STEP], w_fc1_ref.at[:, c : c + FF_STEP], sems.at[n]
        )
        for n, c in enumerate(range(0, hidden, FF_STEP))
    ]
    x_copies, mid_copies = [], []
    for n, slot in enumerate(slots):
        row = order_ref[slot]
        to = slice(n * span, (n + 1) * span)
        x_copies.append(pltpu.make_async_copy(x_hbm.at[row], x_ref.at[to], row_sems.at[0, n]))
        x_copies.append(
            pltpu.make_async_copy(d_out_hbm.at[row], d_out_ref.at[to], row_sems.at[1, n])
        )
        rows = pl.ds(pl.multiple_of(row * span, span), span)
        mid_copies.append(
            pltpu.make_async_copy(d_mid_hbm.at[rows], d_mid_ref.at[to], row_sems.at[2, n])
        )
    for copy in x_copies + weight_copies + mid_copies:
        copy.start()

    for n in range(count):
        for s in range(group):
            scaled_ref[n * span : (n + 1) * span, s * width : (s + 1) * width] = o_refs[n][s, 0]
    proj_hat, proj_spread = norm_parts(dot(scaled_ref[...], w_out_ref[...]))
    for copy in x_copies:
        copy.wait()
    residual = x_ref[...].astype(F32) + proj_hat * post_ref[...]
    residual_ref[...] = residual
    res_hat, res_spread = norm_parts(residual)
    ffn_in = (res_hat * ffn_ref[...]).astype(BF16)
    ffn_in_ref[...] = ffn_in

    total = jnp.zeros((tokens, 1), F32)
    for n, at in enumerate(steps):
        if n % count == 0:
            weight_copies[n // count].wait()
        pre = dot(ffn_in, w_fc1_ref[:, at])
        phi = 0.5 + 0.5 * lax.erf(pre * (0.5**0.5))
        act = pre * phi
        act_ref[:, at] = act
        slope = phi + pre * jnp.exp(-0.5 * pre * pre) * 0.3989422804014327
        slope_ref[:, at] = slope.astype(slope_ref.dtype)
        total += jnp.sum(act, axis=1, keepdims=True)
    average = total / hidden
    total = jnp.zeros((tokens, 1), F32)
    for at in steps:
        centred = act_ref[:, at] - average
        total += jnp.sum(centred * centred, axis=1, keepdims=True)
    spread = lax.rsqrt(total / hidden + EPSILON)

    for copy in mid_copies:
        copy.wait()
    sum_weighted = jnp.zeros((tokens, 1), F32)
    sum_hat = jnp.zeros((tokens, 1), F32)
    for at in steps:
        hat = (act_ref[:, at] - average) * spread
        act_ref[:, at] = hat
        gain = mid_gain_ref[:, at]
        mid_ref[:, at] = (hat * gain).astype(BF16)
        grad = d_mid_ref[:, at]
        product = grad * hat
        g_mid_ref[:, at] = jnp.sum(product, axis=0, keepdims=True)
        sum_weighted += jnp.sum(grad * gain, axis=1, keepdims=True)
        sum_hat += jnp.sum(product * gain, axis=1, keepdims=True)
    sum_weighted = sum_weighted / hidden
    sum_hat = sum_hat / hidden
    d_ffn = jnp.zeros(x_ref.shape, F32)
    for at in steps:
        weighted = d_mid_ref[:, at] * mid_gain_ref[:, at]
        d_act = spread * (weighted - sum_weighted - act_ref[:, at] * sum_hat)
        d_pre = (d_act * slope_ref[:, at].astype(F32)).astype(BF16)
        d_pre_ref[:, at] = d_pre
        d_ffn += dot_last(d_pre, w_fc1_ref[:, at])

    g_ffn_ref[...] = jnp.sum(d_ffn * res_hat, axis=0, keepdims=True)
    d_residual = d_out_ref[...].astype(F32) + norm_back(res_hat, res_spread, ffn_ref[...], d_ffn)
    d_residual_ref[...] = d_residual
    g_post_ref[...] = jnp.sum(d_residual * proj_hat, axis=0, keepdims=True)
    d_proj = norm_back(proj_hat, proj_spread, post_ref[...], d_residual).astype(BF16)
    d_proj_ref[...] = d_proj
    d_attn = (dot_last(d_proj, w_out_ref[...]) * scale_ref[...]).astype(BF16)
    for n in range(count):
        for s in range(group):
            d_attn_ref[s, n] = d_attn[n * span : (n + 1) * span, s * width : (s + 1) * width]


def layer(order, slots, blocks, x, d_out, gains, w_out, d_mid, w_fc1):
    group, _, span, width = blocks[0][0].shape
    model, hidden = w_fc1.shape
    tokens = len(slots) * span
    shape = jax.ShapeDtypeStruct

    def block_spec(at):
        return pl.BlockSpec((group, 1, span, width), lambda i, o: (0, at, 0, 0))

    return pl.pallas_call(
        functools.partial(layer_kernel, slots),
        grid_spec=pltpu.PrefetchScalarGridSpec(
            num_scalar_prefetch=1,
            grid=(1,),
            in_specs=[VMEM] * 5
            + [pl.BlockSpec(memory_space=pl.ANY)] * 4
            + [block_spec(at) for _, at in blocks],
            out_specs=[VMEM] * 11,
            scratch_shapes=[
                pltpu.VMEM((tokens, model), BF16),
                pltpu.VMEM((tokens, model), BF16),
                pltpu.VMEM((tokens, hidden), d_mid.dtype),
                pltpu.VMEM(w_fc1.shape, BF16),
                pltpu.VMEM((tokens, hidden), F32),
                pltpu.VMEM((tokens, hidden), F32 if len(slots) == 1 else BF16),
                pltpu.SemaphoreType.DMA((hidden // FF_STEP,)),
                pltpu.SemaphoreType.DMA((3, len(slots))),
            ],
        ),
        out_shape=[
            shape((tokens, model), BF16),
            shape((tokens, model), BF16),
            shape((tokens, model), F32),
            shape((tokens, hidden), BF16),
            shape((tokens, hidden), BF16),
            shape((tokens, model), BF16),
            shape((tokens, model), F32),
            shape((group, len(slots), span, width), BF16),
            shape((1, model), F32),
            shape((1, model), F32),
            shape((1, hidden), F32),
        ],
        compiler_params=pltpu.CompilerParams(vmem_limit_bytes=LAYER_VMEM),
        cost_estimate=cost(0, 1024),
        name="layer",
    )(order, *gains, w_out, x, d_out, d_mid, w_fc1, *[block for block, _ in blocks])


def layer_out_kernel(order_ref, *refs):
    count = (len(refs) - 2) // 2
    weight, out_ref = refs[-2], refs[-1]
    span, slot = out_ref.shape[1], 0
    for n in range(count):
        result = (refs[n][...] + dot(refs[count + n][...], weight[...])).astype(BF16)
        for at in range(0, result.shape[0], span):
            out_ref[order_ref[slot]] = result[at : at + span]
            slot += 1


def last_step(order, shape, residuals, mids, w_fc2):
    return pl.pallas_call(
        layer_out_kernel,
        in_specs=[SMEM] + [VMEM] * (2 * len(mids) + 1),
        out_shape=jax.ShapeDtypeStruct(shape, BF16),
        compiler_params=kernel_params(),
        cost_estimate=cost(0, 1024),
        name="layer_out",
    )(order, *residuals, *mids, w_fc2)


def flip(value, axis, bit):
    size = lax.axis_size(axis)
    return lax.ppermute(value, axis, [(i, i ^ (1 << bit)) for i in range(size)])


def bits(axis):
    return (lax.axis_size(axis) - 1).bit_length()


PARTS = 4


def weight_kernel(count, rows, added, shards, part_ref, *refs):
    out_ref = refs[-1]
    high = out_ref.shape[1]
    per = rows * (shards + 1)
    extras = refs[per * count : per * count + added]
    at = 0
    for n in range(count):
        mine = refs[n * per : (n + 1) * per]
        rights = mine[rows * shards :]
        width = rights[0].shape[1]
        total = 0.0
        for r in range(rows):
            left = [ref[...] for ref in mine[r * shards : (r + 1) * shards]]
            left = jnp.concatenate(left, axis=1) if shards > 1 else left[0]
            total += dot_first(left, rights[r][...])
        for i in range(shards):
            piece = total[i * high : (i + 1) * high]
            for extra in extras:
                piece = piece + extra[i, :, at : at + width].astype(F32)
            out_ref[i, :, at : at + width] = piece.astype(BF16)
        at += width


def weight_part_plain(pairs, part, parts, extras, group):
    pieces = []
    for lefts, rights, kind in pairs:
        left, right = jnp.concatenate(lefts), jnp.concatenate(rights)
        if kind == "columns":
            wide = right.shape[1] // parts
            right = lax.dynamic_slice(right, (0, part * wide), (right.shape[0], wide))
            left = left.reshape(left.shape[0], group, -1)
        else:
            left = left.reshape(left.shape[0], group, parts, -1)
            left = lax.dynamic_index_in_dim(left, part, 2, keepdims=False)
        pieces.append(jnp.einsum("tsd,te->sde", left, right, preferred_element_type=F32))
    total = jnp.concatenate(pieces, axis=2)
    axis = 2 if pairs[0][2] == "columns" else 1
    for extra, at in extras:
        size = total.shape[axis]
        total = total + lax.dynamic_slice_in_dim(extra, at * size, size, axis).astype(F32)
    return total.astype(BF16)


def weight_part(pairs, part, parts, extras, group):
    shards = 2
    specs, arrays, width = [], [], 0
    for lefts, rights, kind in pairs:
        model = lefts[0].shape[1]
        stride = 1 if kind == "columns" else parts
        high = model // group // stride
        wide = rights[0].shape[1] // (parts if kind == "columns" else 1)
        for left in lefts:
            for i in range(shards):

                def left_at(g, p, i=i, stride=stride):
                    return (0, (g * shards + i) * stride + (p[0] if stride > 1 else 0))

                specs.append(pl.BlockSpec((left.shape[0], high), left_at))
                arrays.append(left)
        for right in rights:

            def right_at(g, p, stride=stride):
                return (0, p[0] if stride == 1 else 0)

            specs.append(pl.BlockSpec((right.shape[0], wide), right_at))
            arrays.append(right)
        width += wide
    if high % 128:
        return weight_part_plain(pairs, part, parts, extras, group)
    block = pl.BlockSpec((shards, high, width), lambda g, p: (g, 0, 0))
    by_row = pairs[0][2] == "rows"

    def extra_spec(n):
        def block_at(g, p):
            return (g, p[n], 0) if by_row else (g, 0, p[n])

        return pl.BlockSpec((shards, high, width), block_at)

    numbers = jnp.stack([part] + [at for _, at in extras]).astype(jnp.int32)
    return pl.pallas_call(
        functools.partial(weight_kernel, len(pairs), len(pairs[0][0]), len(extras), shards),
        grid_spec=pltpu.PrefetchScalarGridSpec(
            num_scalar_prefetch=1,
            grid=(group // shards,),
            in_specs=specs + [extra_spec(n + 1) for n in range(len(extras))],
            out_specs=block,
        ),
        out_shape=jax.ShapeDtypeStruct((group, high, width), BF16),
        compiler_params=kernel_params(),
        cost_estimate=cost(0, 1024),
        name="weight_part",
    )(numbers, *arrays, *[extra for extra, _ in extras])


class WeightSum:
    def __init__(self, *pairs):
        self.pairs = pairs
        batch_at = lax.axis_index("batch")
        self.near, self.far = batch_at & 1, (batch_at >> 1) & 1
        self.zero = batch_at * 0

    def piece(self, order, near, far, *extras):
        def part_of(part):
            return weight_part(self.pairs, part, PARTS, extras, lax.axis_size("blk"))

        return order(part_of, near * 2 + far)

    def half(self, order, near, *extras):
        def part_of(part):
            return weight_part(self.pairs, part, 2, extras, lax.axis_size("blk"))

        return order(part_of, near)

    def away_far(self, order):
        return self.piece(order, 1 - self.near, 1 - self.far)

    def away_near(self, order):
        return self.piece(order, 1 - self.near, self.far)

    def away(self, order, *more):
        return self.half(order, 1 - self.near, *more)

    def send_far(self, order, away):
        return self.piece(order, self.near, 1 - self.far, (away, self.zero))

    def send(self, order, *aways):
        extras = [(away, 1 - self.far) for away in aways]
        return self.piece(order, self.near, 1 - self.far, *extras)

    def keep(self, order, near, arrived):
        return self.piece(order, self.near, self.far, (near, self.zero), (arrived, self.zero))

    def keep_rest(self, order, arrived, *aways):
        extras = [(away, self.far) for away in aways]
        return self.piece(order, self.near, self.far, (arrived, self.zero), *extras)

    def own(self, order, *aways):
        return self.half(order, self.near, *[(away, self.zero) for away in aways])


def over_near(sent):
    return flip(sent, "batch", 0)


def over_far(sent):
    return flip(sent, "batch", 1)


class Order:
    def __init__(self):
        self.last = ()

    def __call__(self, step, *values):
        self.last = step(*tie(values, self.last))
        return self.last


def window(always, step):
    def nothing():
        return jax.tree.map(lambda leaf: jnp.zeros(leaf.shape, leaf.dtype), jax.eval_shape(step))

    return lax.cond(always, step, nothing)


def tie(values, *after):
    return lax.optimization_barrier((values, after))[0]


def combine_kernel(plan, at_ref, *refs):
    ins = sum(count for _, count, _ in plan)
    into, out_of = list(refs[:ins]), list(refs[ins:])
    for n, (kind, count, cut) in enumerate(plan):
        terms = [into.pop(0) for _ in range(count)]
        if kind == "small":
            out_of.pop(0)[...] = sum(term[...] for term in terms)
            continue
        if kind == "stack":
            out = out_of.pop(0)
            out[0], out[1] = terms[0][0], terms[1][0]
            continue

        def put(ref, j, i):
            if kind == "add":
                ref[j] = (terms[0][i].astype(F32) + terms[1][i].astype(F32)).astype(BF16)
                return
            at = 0
            for term in terms:
                ref[j, :, at : at + term.shape[2]] = term[i]
                at += term.shape[2]

        if cut:
            keep, send = out_of.pop(0), out_of.pop(0)
            for j in range(keep.shape[0]):
                put(keep, j, 2 * j + at_ref[n])
                put(send, j, 2 * j + 1 - at_ref[n])
        else:
            whole = out_of.pop(0)
            for j in range(whole.shape[0]):
                put(whole, j, j)


class Tree:
    def __init__(self, *mine, halved=2):
        self.steps = [("blk", bit) for bit in range(bits("blk"))]
        self.steps += [("batch", bit) for bit in range(halved, bits("batch"))]
        self.steps += [("far", 1), ("near", 0)][2 - halved :]
        self.terms, self.last = list(mine), "first"

    def start(self):
        kind, bit = self.steps[0]
        return flip(self.send, "blk" if kind == "blk" else "batch", bit)

    def end(self, arrived):
        self.last = self.steps.pop(0)[0]
        self.terms = [self.kept, arrived]


def combine(trees):
    me = lax.axis_index("blk")
    plan, ins, shapes, at = [], [], [], []
    for tree in trees:
        kind, bit = tree.steps[0]
        cut = kind == "blk" and tree.last != "small"
        if tree.last == "small":
            plan.append(("small", len(tree.terms), False))
            ins += tree.terms
            shapes.append(jax.ShapeDtypeStruct(tree.terms[0].shape, F32))
            at.append(me * 0)
            continue
        state = {"first": "first", "far": "stack"}.get(tree.last, "add")
        plan.append((state, len(tree.terms), cut))
        ins += tree.terms
        count, high, wide = tree.terms[0].shape
        if state == "first":
            wide = sum(term.shape[2] for term in tree.terms)
        count = count // 2 if cut else 2 if state == "stack" else count
        shapes += [jax.ShapeDtypeStruct((count, high, wide), BF16)] * (2 if cut else 1)
        at.append((me >> bit) & 1 if cut else me * 0)
    outs = list(
        pl.pallas_call(
            functools.partial(combine_kernel, plan),
            in_specs=[SMEM] + [VMEM] * len(ins),
            out_shape=shapes,
            compiler_params=kernel_params(),
            cost_estimate=cost(0, 1024),
            name="combine",
        )(jnp.stack(at).astype(jnp.int32), *ins)
    )
    for tree, (_, _, cut) in zip(trees, plan):
        tree.kept = outs.pop(0)
        tree.send = outs.pop(0) if cut else tree.kept


def place_kernel(layout, lines, part_ref, *refs):
    count = 2 * len(layout) + (2 if lines else 0)
    ins, outs = list(refs[:count]), list(refs[count:])
    if lines:
        one, other = ins[-2:]
        for (start, size, cut), out in zip(lines, outs[-len(lines) :]):
            at = pl.ds(start, size)
            if cut:
                at = pl.ds(pl.multiple_of(start + part_ref[2] * size, 128), size)
            out[...] = one[:, at] + other[:, at]
    near, far = part_ref[0], part_ref[1]
    order = [near * 2 + far, near * 2 + 1 - far, (1 - near) * 2 + far, (1 - near) * 2 + 1 - far]
    for spans in layout:
        both = [ins.pop(0), ins.pop(0)]
        count = 2 * both[0].shape[0]
        for start, width, kind in spans:
            out = outs.pop(0)
            for n, part in enumerate(order if count == 4 else [near, 1 - near]):
                value = both[n * 2 // count][n % (count // 2), :, start : start + width]
                value = value.astype(F32)
                if kind == "columns":
                    out[:, pl.ds(pl.multiple_of(part * width, 128), width)] = value
                else:
                    high = value.shape[0]
                    out[pl.ds(pl.multiple_of(part * high, 8), high), :] = value


def place(trees, layout, small=None, lines=()):
    batch_at = lax.axis_index("batch")
    parts = jnp.stack([batch_at & 1, (batch_at >> 1) & 1, lax.axis_index("blk")])
    parts = parts.astype(jnp.int32)
    ins, shapes = [], []
    for tree, spans in zip(trees, layout):
        ins += tree.terms
        count, high = 2 * tree.kept.shape[0], tree.kept.shape[1]
        for _, width, kind in spans:
            shape = (high, count * width) if kind == "columns" else (count * high, width)
            shapes.append(jax.ShapeDtypeStruct(shape, F32))
    if lines:
        ins += small.terms
        shapes += [jax.ShapeDtypeStruct((1, size), F32) for _, size, _ in lines]
    return pl.pallas_call(
        functools.partial(place_kernel, layout, lines),
        in_specs=[SMEM] + [VMEM] * len(ins),
        out_shape=shapes,
        compiler_params=kernel_params(),
        cost_estimate=cost(0, 1024),
        name="place",
    )(parts, *ins)


class SmallSum:
    def __init__(self, mine):
        self.steps = [("batch", bit) for bit in range(bits("batch"))]
        self.steps += [("blk", bit) for bit in range(bits("blk"))]
        self.terms, self.last = [mine], "small"

    def start(self):
        return flip(self.send, *self.steps[0])

    def end(self, arrived):
        self.steps.pop(0)
        self.terms = [self.kept, arrived]


def input_grad_kernel(parts, order_ref, x_ref, gain_ref, wq_ref, wk_ref, wv_ref, *refs):
    out_ref, sum_ref = refs[-2:]
    rows, span, model = x_ref.shape
    piece = model // parts
    total = jnp.zeros(sum_ref.shape, F32)
    residuals = [
        held.at[pl.ds(at, span)] for held in refs[2 * rows : -2] for at in range(0, held.shape[0], span)
    ]
    for r in range(rows):
        d_ref, value_ref, res_ref = refs[r], refs[rows + r], residuals[r]
        grad = dot_last(value_ref[...], wv_ref[...])
        for p in range(parts):
            for n, weight in enumerate((wq_ref, wk_ref)):
                at = (p * 2 + n) * piece
                grad += dot_last(d_ref[:, at : at + piece], weight[:, p * piece : (p + 1) * piece])
        row = order_ref[r]
        hat, spread = norm_parts(x_ref[row].astype(F32))
        out_ref[row] = res_ref[...] + norm_back(hat, spread, gain_ref[...], grad)
        total += jnp.sum(grad * hat, axis=0, keepdims=True)
    sum_ref[...] = total


def input_grad(order, x, gain, w_query, w_key, w_value, d_rows, d_values, d_residuals):
    return pl.pallas_call(
        functools.partial(input_grad_kernel, PARTS),
        in_specs=[SMEM] + [VMEM] * (5 + 2 * len(d_rows) + len(d_residuals)),
        out_shape=[
            jax.ShapeDtypeStruct(x.shape, F32),
            jax.ShapeDtypeStruct((1, x.shape[2]), F32),
        ],
        compiler_params=kernel_params(),
        cost_estimate=cost(0, 1024),
        name="input_grad",
    )(order, x, gain, w_query, w_key, w_value, *d_rows, *d_values, *d_residuals)


def on_device(
    inputs,
    ln_attn,
    w_query,
    w_key,
    w_value,
    w_out,
    head_scale,
    ln_post,
    ln_ffn,
    w_fc1,
    ln_mid,
    w_fc2,
    offsets,
    cotangent,
):
    row_count, span, model = inputs.shape
    head_count = head_scale.shape[0]
    head_dim = model // head_count
    tokens = row_count * span
    group = lax.axis_size("blk")
    heads = head_count // group
    width = heads * head_dim
    my_index = lax.axis_index("blk")
    rows = range(row_count)

    always = offsets[0, 0] == 0
    gain = ln_attn.reshape(1, model)
    last = row_count - 1
    my_scale = lax.dynamic_slice(head_scale, (my_index * heads,), (heads,))
    scale_lanes = jnp.repeat(my_scale, head_dim).reshape(1, width)
    layer_gains = [
        ln_post.reshape(1, model),
        ln_ffn.reshape(1, model),
        ln_mid.reshape(1, -1),
        jnp.repeat(head_scale, head_dim).reshape(1, model),
    ]

    def project_row(r, x):
        return project(offsets, r, x, gain, w_query, w_key, w_value, group)

    def attend_one(r, held, into=None):
        place = (r, last) if r < last else (0, 1)
        return attend(by_work, offsets, r, held, scale_lanes, heads, head_dim, *place, into)

    def layer_rows(slots, blocks):
        return layer(by_work, slots, blocks, inputs, cotangent, layer_gains, w_out, d_mid, w_fc1)

    def back(order, r, row_heads, at=0):
        def back_row(held):
            return attend_back(
                by_work,
                offsets,
                r,
                held,
                row_heads,
                at,
                *((first_out, r) if r < last else (last_out, 0)),
                1.0 / scale_lanes,
                lse[r],
                heads,
                head_dim,
            )

        return order(back_row, qkv[r])

    def first_window():
        order = Order()
        return exchange(sent), [
            order(functools.partial(project_row, r), inputs) for r in rows[1:]
        ]

    normed_first, sent, by_work = project_row(0, inputs)
    held, projected = first_window()
    qkv = [held]
    normed = [normed_first] + [part[0] for part in projected]
    first_out, lse = None, []
    for r in rows[1:]:

        def next_window():
            order = Order()
            extra = ()
            if r == 1:
                d_mid = jnp.einsum(
                    "td,fd->tf",
                    cotangent.reshape(tokens, model),
                    w_fc2,
                    preferred_element_type=F32,
                )
                extra = d_mid
            if r == last:
                d_out = [
                    lax.dynamic_index_in_dim(cotangent, by_work[n], keepdims=False) for n in rows
                ]
                extra = d_out[0], jnp.concatenate(d_out[1:])
            return exchange(projected[r - 1][1]), attend_one(r - 1, qkv[r - 1], first_out), extra

        held, (first_out, log_total), extra = window(always, next_window)
        d_mid = extra if r == 1 else d_mid
        qkv.append(held)
        lse.append(log_total)

    d_out = list(extra)

    def early_window():
        return (
            exchange(first_out),
            attend_one(last, qkv[last]),
        )

    early, (last_out, log_total) = window(always, early_window)
    lse.append(log_total)

    def late_window():
        return exchange(last_out), layer_rows([0], [(early, 0)])

    late, layer_first = window(always, late_window)

    def layer_window():
        blocks = [(early, r) if r < last else (late, 0) for r in rows[1:]]
        return exchange(layer_first[7]), layer_rows(list(rows[1:]), blocks)

    first_heads, layer_rest = window(always, layer_window)
    (
        scaled,
        ffn_in,
        residual,
        mid,
        d_pre,
        d_proj,
        d_residual,
        d_attn,
        g_post,
        g_ffn,
        g_mid,
    ) = zip(layer_first, layer_rest)
    sum_one = WeightSum((mid, d_out, "rows"))
    sum_two = WeightSum((ffn_in, d_pre, "columns"))
    sum_three = WeightSum((scaled, d_proj, "columns"))
    order = Order()
    away_one = over_near(sum_one.away_far(order))
    near_one = over_near(sum_one.away_near(order))
    far_one = over_far(sum_one.send_far(order, away_one))

    def back_first():
        order = Order()
        heads_in = exchange(d_attn[1])
        away = over_near(sum_two.away_far(order))
        out = back(order, 0, first_heads)
        return heads_in, out, sum_two.send_far(order, away)

    rest_heads, (sent, total), sent_two = window(always, back_first)
    far_two = over_far(sent_two)
    totals = [total]

    def back_second():
        order = Order()
        grad = exchange(sent)
        out = back(order, 1, rest_heads, 0)
        near = sum_two.away_near(order), sum_three.away(order)
        return grad, out, near, sum_one.keep(order, near_one, far_one)

    grad, (sent, total), near, mine_one = window(always, back_second)
    near_two, away_three = near
    totals.append(total)
    grads = [grad]
    tree_one = Tree(mine_one)
    combine([tree_one])
    moved = tree_one.start()
    sent = tie(sent, tree_one.send)
    near_two, away_three = over_near(near_two), over_near(away_three)
    for r in rows[2:]:

        def back_next():
            order = Order()
            out_of = ()
            grad = exchange(sent)
            out = back(order, r, rest_heads, r - 1)
            if r == 2:
                mine = sum_two.keep(order, near_two, far_two)
                out_of = mine, sum_three.own(order, away_three)
            return grad, out_of, out

        grad, out_of, (sent, total) = window(always, back_next)
        totals.append(total)
        grads.append(grad)
        if r == 2:
            mine_two, mine_three = out_of
    tree_one.end(moved)
    tree_two = Tree(mine_two)
    combine([tree_one, tree_two])

    moved = tree_one.start(), tree_two.start()
    sent = tie(sent, tree_one.send, tree_two.send)

    def back_last():
        order = Order()
        grad = exchange(sent)
        joined = [order(join_grads, part) for part in grads]

        def output_step(weight):
            return last_step(by_work, inputs.shape, residual, mid, weight)

        d_rows, d_values = zip(*joined)
        early_qk = WeightSum((normed[:last], d_rows, "columns"))
        early_v = WeightSum((normed[:last], d_values, "columns"))
        early = [early_qk.away(order), early_v.away(order), early_qk.own(order), early_v.own(order)]
        return grad, joined, order(output_step, w_fc2), early

    grad, joined, layer_out, early_sums = window(always, back_last)
    early_away_qk, early_away_v, early_qk, early_v = early_sums
    grad, moved = tie((grad, moved))
    tree_one.end(moved[0])
    tree_two.end(moved[1])
    order = Order()
    joined = joined + [order(join_grads, grad)]
    d_rows, d_values = zip(*joined)
    sum_qk = WeightSum((normed[last:], d_rows[last:], "columns"))
    sum_v = WeightSum((normed[last:], d_values[last:], "columns"))
    away_qk = over_near(sum_qk.away(order, (early_away_qk, sum_qk.zero)))
    away_v = over_near(sum_v.away(order, (early_away_v, sum_v.zero)))
    sent_qk = sum_qk.send(order, away_qk, early_qk)
    tree_v = Tree(sum_v.own(order, away_v, early_v), mine_three, halved=1)
    combine([tree_one, tree_two, tree_v])

    def advance(trees, extra=lambda: ()):
        def step():
            return [tree.start() for tree in trees], extra()

        moved, out = window(always, step)
        for tree, arrived in zip(trees, moved):
            tree.end(arrived)
        return out

    def beside():
        order = Order()
        arrived = over_far(sent_qk)

        def input_step(x):
            return input_grad(
                by_work, x, gain, w_query, w_key, w_value, d_rows, d_values, d_residual
            )

        return arrived, order(input_step, inputs)

    far_qk, (grad_inputs, grad_ln_attn) = advance(
        [tree_one, tree_two, tree_v], beside
    )
    tree_qk = Tree(sum_qk.keep_rest(order, far_qk, away_qk, early_qk))
    delta_sum = sum(jnp.sum(total, axis=1) for total in totals)
    my_grad = delta_sum[:heads] / my_scale
    scale_part = lax.dynamic_update_slice(
        jnp.zeros((head_count,), F32), my_grad, (my_index * heads,)
    )
    small = SmallSum(
        jnp.concatenate(
            [grad_ln_attn[0], sum(g_post)[0], sum(g_ffn)[0], sum(g_mid)[0], scale_part]
        ).reshape(1, -1)
    )
    piece = model // PARTS
    ff_piece = w_fc1.shape[1] // PARTS
    trees = [tree_qk, tree_v, tree_two, tree_one]
    placed = None
    while any(tree.steps for tree in trees + [small]):
        combine([tree for tree in trees + [small] if tree.steps])

        def place_early():
            if tree_two.steps or tree_one.steps or placed is not None:
                return ()
            return place(
                [tree_one, tree_two], [[(0, model, "rows")], [(0, ff_piece, "columns")]]
            )

        early_out = advance([tree for tree in trees + [small] if tree.steps], place_early)
        placed = early_out or placed
    if placed is None:
        placed = place([tree_one, tree_two], [[(0, model, "rows")], [(0, ff_piece, "columns")]])
    grad_fc2, grad_fc1 = placed
    lines = [(0, model), (model, model), (2 * model, model), (3 * model, ln_mid.shape[0])]
    ends = lines[-1][0] + lines[-1][1]
    layout = [
        [(n * piece, piece, "columns") for n in range(2)],
        [(n * 2 * piece, 2 * piece, "columns") for n in range(2)],
    ]
    if model // group % 128:
        grad_query, grad_key, grad_value, grad_out = place([tree_qk, tree_v], layout)
        total = sum(small.terms)[0]
        gains = [
            lax.dynamic_slice(total, (start + my_index * (size // group),), (size // group,))
            for start, size in lines
        ]
        gains.append(total[ends:])
    else:
        lines = [(start, size // group, True) for start, size in lines]
        lines.append((ends, head_count, False))
        grad_query, grad_key, grad_value, grad_out, *gains = place(
            [tree_qk, tree_v], layout, small, lines
        )
        gains = [line[0] for line in gains]
    return (
        layer_out,
        grad_inputs,
        gains[0],
        grad_query,
        grad_key,
        grad_value,
        grad_out,
        gains[4],
        gains[1],
        gains[2],
        grad_fc1,
        gains[3],
        grad_fc2,
    )


def solution(mesh):
    rows = P("batch", "blk", None)
    shard = P("blk", None)
    return jax.shard_map(
        on_device,
        mesh=mesh,
        in_specs=(rows,) + (P(),) * 11 + (P("batch", None), rows),
        out_specs=(
            rows,
            rows,
            P("blk"),
            shard,
            shard,
            shard,
            shard,
            P(),
            P("blk"),
            P("blk"),
            shard,
            P("blk"),
            shard,
        ),
        check_vma=False,
    )
```

profile of v0, /device:TPU:0, one launch (start us, length us, event | category | flops | bytes accessed | tf_op | source)
XLA Modules:
  0.0 548.7 jit_solution(2520663944964441074)
XLA Ops:
  26.7 24.4 %all-to-all-done.9 = bf16[8,3,256,128]{3,2,1,0:T(8,128)(2,1)} async-done(((bf16[8,3,256,128]{3,2,1,0:T(8,128)(2,1)}), bf16[8,3,256,128]{3,2,1,0:T(8,128)(2,1)}, u32[]{:S(2)}, u32[]{:S(2)}) %all-to-all-start.9) | async-done | bytes 1572896 | tf_op jit(solution)/shard_map/all_to_all | solution.py:42
  51.0 41.1 %conditional.15 = (bf16[8,3,256,128]{3,2,1,0:T(8,128)(2,1)}, bf16[8,2,256,128]{3,2,1,0:T(8,128)(2,1)S(1)}, f32[8,2,256]{2,1,0:T(2,128)S(1)}, f32[768,4096]{1,0:T(8,128)}) conditional(s32[]{:T(128)} %bitcast.22, () %tuple.169, (bf16[8,3,256,128]{3,2,1,0:T(8,128)(2,1)}, s32[3]{0:T(128)S(1)}, s32[3,4]{1,0:T(4,128)S(1)}, f32[1,128]{1,0:T(1,128)S(1)}, ...), branch_computations={%region_0.0_spmd, %region_1.0_spmd} | conditional | flops 6442450944 | bytes 33555548 | solution.py:785
  55.5 19.4 %attend.3 = (bf16[8,2,256,128]{3,2,1,0:T(8,128)(2,1)S(1)}, f32[8,2,256]{2,1,0:T(2,128)S(1)}) custom-call(s32[3]{0:T(128)S(1)} %get-tuple-element.319.order_ref, s32[3,4]{1,0:T(4,128)S(1)} %get-tuple-element.320.offs_ref, f32[1,128]{1,0:T(1,128)S(1)} %get-tuple-element.321.scale_ref, bf16[8,3,256,128]{3,2,1,0:T(8,128)(2,1)} %get-tuple-element.322.held), custom_call_target="tpu_custom_call" | custom-call | bytes 1024 | tf_op jit(solution)/shard_map/cond/branch_1_fun/attend/pallas_call | solution.py:252
  74.9 12.6 %fusion.4 = f32[768,4096]{1,0:T(8,128)} fusion(bf16[768,1024]{1,0:T(8,128)(2,1)S(1)} %bitcast.55, bf16[4096,1024]{1,0:T(8,128)(2,1)} %get-tuple-element.326), kind=kOutput, calls=%fused_computation.32 | convolution fusion | flops 6442450944 | bytes 22544384 | tf_op jit(solution)/shard_map/cond/branch_1_fun/td,fd->tf/dot_general | solution.py:1061
  92.1 41.1 %conditional.16 = (bf16[8,3,256,128]{3,2,1,0:T(8,128)(2,1)}, bf16[8,2,256,128]{3,2,1,0:T(8,128)(2,1)}, f32[8,2,256]{2,1,0:T(2,128)S(1)}, bf16[256,1024]{1,0:T(8,128)(2,1)}, bf16[512,1024]{1,0:T(8,128)(2,1)S(1)}) conditional(s32[]{:T(128)} %bitcast.22, () %tuple.167, (bf16[8,3,256,128]{3,2,1,0:T(8,128)(2,1)}, s32[3]{0:T(128)S(1)}, ...), branch_computations={%region_2.0_spmd, %region_3.4_spmd} | conditional | flops 2097161 | bytes 18351342 | solution.py:785
  100.9 16.0 %attend.4 = (bf16[8,2,256,128]{3,2,1,0:T(8,128)(2,1)S(1)}, f32[8,2,256]{2,1,0:T(2,128)S(1)}) custom-call(s32[3]{0:T(128)S(1)} %get-tuple-element.328.order_ref, s32[3,4]{1,0:T(4,128)S(1)} %get-tuple-element.329.offs_ref, f32[1,128]{1,0:T(1,128)S(1)} %get-tuple-element.330.scale_ref, ...), custom_call_target="tpu_custom_call", output_to_operand_aliasing={{0}: (4, {})} | custom-call | bytes 1024 | tf_op jit(solution)/shard_map/cond/branch_1_fun/attend/pallas_call | solution.py:252
  120.9 12.1 %all-to-all-done.7 = bf16[8,3,256,128]{3,2,1,0:T(8,128)(2,1)} async-done(((bf16[8,3,256,128]{3,2,1,0:T(8,128)(2,1)}), bf16[8,3,256,128]{3,2,1,0:T(8,128)(2,1)}, u32[]{:S(2)}, u32[]{:S(2)}) %all-to-all-start.7) | async-done | bytes 1572896 | tf_op jit(solution)/shard_map/cond/branch_1_fun/all_to_all | solution.py:42
  134.2 29.9 %conditional.17 = (bf16[8,2,256,128]{3,2,1,0:T(8,128)(2,1)}, bf16[8,1,256,128]{3,2,1,0:T(8,128)(2,1)}, f32[8,2,256]{2,1,0:T(2,128)S(1)}) conditional(s32[]{:T(128)} %bitcast.22, () %tuple.166, (bf16[8,2,256,128]{3,2,1,0:T(8,128)(2,1)}, s32[3]{0:T(128)S(1)}, s32[3,4]{1,0:T(4,128)S(1)}, f32[1,128]{1,0:T(1,128)S(1)}, ...), branch_computations={%region_4.5_spmd, %region_5.6_spmd} | conditional | bytes 3146808 | solution.py:785
  138.5 16.0 %attend.5 = (bf16[8,1,256,128]{3,2,1,0:T(8,128)(2,1)}, f32[8,2,256]{2,1,0:T(2,128)S(1)}) custom-call(s32[3]{0:T(128)S(1)} %get-tuple-element.337.order_ref, s32[3,4]{1,0:T(4,128)S(1)} %get-tuple-element.338.offs_ref, f32[1,128]{1,0:T(1,128)S(1)} %get-tuple-element.339.scale_ref, bf16[8,3,256,128]{3,2,1,0:T(8,128)(2,1)} %get-tuple-element.340.held), custom_call_target="tpu_custom_call" | custom-call | bytes 1024 | tf_op jit(solution)/shard_map/cond/branch_1_fun/attend/pallas_call | solution.py:252
  164.1 22.0 %conditional.18 = (bf16[8,1,256,128]{3,2,1,0:T(8,128)(2,1)}, bf16[256,1024]{1,0:T(8,128)(2,1)}, bf16[256,1024]{1,0:T(8,128)(2,1)}, f32[256,1024]{1,0:T(8,128)}, ...) conditional(s32[]{:T(128)} %bitcast.22, () %tuple.165, ...), branch_computations={%region_6.7_spmd, %region_7.8_spmd} | conditional | bytes 8937602 | solution.py:785
  168.7 17.2 %layer.2 = (bf16[256,1024]{1,0:T(8,128)(2,1)}, bf16[256,1024]{1,0:T(8,128)(2,1)}, f32[256,1024]{1,0:T(8,128)}, bf16[256,4096]{1,0:T(8,128)(2,1)}, bf16[256,4096]...) custom-call(s32[3]{0:T(128)S(1)} %get-tuple-element.344.order_ref, ...), custom_call_target="tpu_custom_call" | custom-call | bytes 1024 | tf_op jit(solution)/shard_map/cond/branch_1_fun/layer/pallas_call | solution.py:551
  186.1 34.0 %conditional.19 = (bf16[8,1,256,128]{3,2,1,0:T(8,128)(2,1)}, bf16[512,1024]{1,0:T(8,128)(2,1)}, bf16[512,1024]{1,0:T(8,128)(2,1)S(1)}, f32[512,1024]{1,0:T(8,128...) conditional(s32[]{:T(128)} %bitcast.22, () %tuple.164, ...), branch_computations={%region_8.9_spmd, %region_9.10_spmd} | conditional | bytes 17326210 | solution.py:785
  192.1 27.6 %layer.3 = (bf16[512,1024]{1,0:T(8,128)(2,1)}, bf16[512,1024]{1,0:T(8,128)(2,1)S(1)}, f32[512,1024]{1,0:T(8,128)}, bf16[512,4096]{1,0:T(8,128)(2,1)}, bf16[512,4...) custom-call(s32[3]{0:T(128)S(1)} %get-tuple-element.367.order_ref, ...), custom_call_target="tpu_custom_call" | custom-call | bytes 1024 | tf_op jit(solution)/shard_map/cond/branch_1_fun/layer/pallas_call | solution.py:551
  239.4 43.2 %conditional.20 = (bf16[8,2,256,128]{3,2,1,0:T(8,128)(2,1)}, bf16[8,1,3,256,128]{4,3,2,1,0:T(8,128)(2,1)}, bf16[8,128,1024]{2,1,0:T(8,128)(2,1)}, f32[8]{0:T(128)S(1)}) conditional(s32[]{:T(128)} %bitcast.22, () %tuple.163, (bf16[8,2,256,128]{3,2,1,0:T(8,128)(2,1)}, f32[1,128]{1,0:T(1,128)S(1)}, s32[]{:T(128)}, s32[]{:T(128)}, ...), branch_computations={%region_10.11_spmd, %region_11.0_spmd} | conditional | flops 2176 | bytes 11546852 | solution.py:785
  250.5 25.7 %attend_back.3 = (bf16[8,1,3,256,128]{4,3,2,1,0:T(8,128)(2,1)}, f32[8,256]{1,0:T(8,128)S(1)}) custom-call(s32[3]{0:T(128)S(1)} %get-tuple-element.391.order_ref, s32[3,4]{1,0:T(4,128)S(1)} %get-tuple-element.392.offs_ref, f32[1,128]{1,0:T(1,128)S(1)} %broadcast_divide_fusion.refs_0_, f32[8,2,256]{2,1,0:T(2,128)S(1)} %get-tuple-element.394.refs_1_, ...), custom_call_target="tpu_custom_call" | custom-call | bytes 1024 | tf_op jit(solution)/shard_map/cond/branch_1_fun/attend_back/pallas_call | solution.py:366
  285.7 44.6 %conditional.21 = (bf16[8,1,3,256,128]{4,3,2,1,0:T(8,128)(2,1)}, bf16[8,1,3,256,128]{4,3,2,1,0:T(8,128)(2,1)}, bf16[8,128,1024]{2,1,0:T(8,128)(2,1)}, bf16[8,128...) conditional(s32[]{:T(128)} %bitcast.22, () %tuple.162, ...), branch_computations={%region_13.14_spmd, %region_14.0_spmd} | conditional | flops 2173 | bytes 8388702 | solution.py:785
  291.9 21.7 %attend_back.4 = (bf16[8,1,3,256,128]{4,3,2,1,0:T(8,128)(2,1)}, f32[8,256]{1,0:T(8,128)S(1)}) custom-call(s32[3]{0:T(128)S(1)} %get-tuple-element.409.order_ref, s32[3,4]{1,0:T(4,128)S(1)} %get-tuple-element.410.offs_ref, f32[1,128]{1,0:T(1,128)S(1)} %broadcast_divide_fusion.1.refs_0_, f32[8,2,256]{2,1,0:T(2,128)S(1)} %get-tuple-element.412.refs_1_, ...), custom_call_target="tpu_custom_call" | custom-call | bytes 1024 | tf_op jit(solution)/shard_map/cond/branch_1_fun/attend_back/pallas_call | solution.py:366
  336.4 43.6 %conditional.22 = (bf16[8,1,3,256,128]{4,3,2,1,0:T(8,128)(2,1)}, bf16[8,128,1024]{2,1,0:T(8,128)(2,1)}, bf16[8,128,512]{2,1,0:T(8,128)(2,1)}, bf16[8,1,3,256,128]{4,3,2,1,0:T(8,128)(2,1)}, f32[8]{0:T(128)S(1)}) conditional(s32[]{:T(128)} %bitcast.22, () %tuple.161, (bf16[8,1,3,256,128]{4,3,2,1,0:T(8,128)(2,1)}, s32[]{:T(128)}, s32[]{:T(128)}, ...), branch_computations={%region_16.17_spmd, %region_17.0_spmd} | conditional | flops 2172 | bytes 6291540 | solution.py:785
  342.4 19.7 %attend_back.5 = (bf16[8,1,3,256,128]{4,3,2,1,0:T(8,128)(2,1)}, f32[8,256]{1,0:T(8,128)S(1)}) custom-call(s32[3]{0:T(128)S(1)} %get-tuple-element.440.order_ref, s32[3,4]{1,0:T(4,128)S(1)} %get-tuple-element.441.offs_ref, f32[1,128]{1,0:T(1,128)S(1)} %broadcast_divide_fusion.2.refs_0_, f32[8,2,256]{2,1,0:T(2,128)S(1)} %get-tuple-element.443.refs_1_, ...), custom_call_target="tpu_custom_call" | custom-call | bytes 1024 | tf_op jit(solution)/shard_map/cond/branch_1_fun/attend_back/pallas_call | solution.py:366
  385.0 40.8 %conditional.23 = (bf16[8,1,3,256,128]{4,3,2,1,0:T(8,128)(2,1)}, bf16[256,2048]{1,0:T(8,128)(2,1)}, bf16[256,1024]{1,0:T(8,128)(2,1)}, bf16[256,2048]{1,0:T(8,12...) conditional(s32[]{:T(128)} %bitcast.22, () %tuple.160, ...), branch_computations={%region_19.20_spmd, %region_20.21_spmd} | conditional | flops 5 | bytes 36183312 | solution.py:785
  451.5 26.6 %conditional.24 = (bf16[1,128,1024]{2,1,0:T(8,128)(2,1)}, bf16[2,128,1024]{2,1,0:T(8,128)(2,1)}, bf16[4,128,1024]{2,1,0:T(8,128)(2,1)}, bf16[8,128,512]{2,1,0:T(...) conditional(s32[]{:T(128)} %bitcast.22, () %tuple.183, (bf16[1,128,1024]{2,1,0:T(8,128)(2,1)}, ...), branch_computations={%region_21.22_spmd, %region_22.23_spmd} | conditional | bytes 11535568 | solution.py:785
  484.5 19.0 %conditional.25 = (bf16[4,128,512]{2,1,0:T(8,128)(2,1)}, bf16[2,128,1024]{2,1,0:T(8,128)(2,1)}, bf16[1,128,1024]{2,1,0:T(8,128)(2,1)}, bf16[1,128,1024]{2,1,0:T(8,128)(2,1)}, f32[1,7184]{1,0:T(1,128)}) conditional(s32[]{:T(128)} %bitcast.22, () %tuple.191, (bf16[4,128,512]{2,1,0:T(8,128)(2,1)S(1)}, bf16[2,128,1024]{2,1,0:T(8,128)(2,1)S(1)}, ...), branch_computations={%region_23.24_spmd, %region_24.25_spmd} | conditional | bytes 6406640 | solution.py:785
  489.6 11.7 %collective-permute-done.6 = bf16[1,128,1024]{2,1,0:T(8,128)(2,1)} collective-permute-done((bf16[1,128,1024]{2,1,0:T(8,128)(2,1)S(1)}, bf16[1,128,1024]{2,1,0:T(8,128)(2,1)}, u32[]{:S(2)}, u32[]{:S(2)}) %collective-permute-start.6) | collective-permute-done | bytes 262176 | tf_op jit(solution)/shard_map/cond/branch_1_fun/ppermute | solution.py:614
  505.2 15.5 %conditional.26 = (bf16[2,128,512]{2,1,0:T(8,128)(2,1)}, bf16[1,128,1024]{2,1,0:T(8,128)(2,1)}, bf16[1,128,1024]{2,1,0:T(8,128)(2,1)}, bf16[2,128,1024]{2,1,0:T(8,128)(2,1)}, f32[1,7184]{1,0:T(1,128)}) conditional(s32[]{:T(128)} %bitcast.22, () %tuple.193, (bf16[2,128,512]{2,1,0:T(8,128)(2,1)S(1)}, bf16[1,128,1024]{2,1,0:T(8,128)(2,1)S(1)}, ...), branch_computations={%region_25.26_spmd, %region_26.27_spmd} | conditional | bytes 5358064 | solution.py:785
  (243 shorter events, 337.4 us)
Async XLA Ops:
  6.5 44.5 %all-to-all-start.9 = ((bf16[8,3,256,128]{3,2,1,0:T(8,128)(2,1)}), bf16[8,3,256,128]{3,2,1,0:T(8,128)(2,1)}, u32[]{:S(2)}, u32[]{:S(2)}) async-start(bf16[8,3,256,128]{3,2,1,0:T(8,128)(2,1)} %get-tuple-element.702), calls=%async_computation.9 | async-start | bytes 3145728 | tf_op jit(solution)/shard_map/all_to_all | solution.py:42
  51.0 41.1 %all-to-all-start.8 = ((bf16[8,3,256,128]{3,2,1,0:T(8,128)(2,1)}), bf16[8,3,256,128]{3,2,1,0:T(8,128)(2,1)}, u32[]{:S(2)}, u32[]{:S(2)}) async-start(bf16[8,3,256,128]{3,2,1,0:T(8,128)(2,1)} %get-tuple-element.318), calls=%async_computation.8 | async-start | bytes 3145728 | tf_op jit(solution)/shard_map/cond/branch_1_fun/all_to_all | solution.py:42
  92.1 40.9 %all-to-all-start.7 = ((bf16[8,3,256,128]{3,2,1,0:T(8,128)(2,1)}), bf16[8,3,256,128]{3,2,1,0:T(8,128)(2,1)}, u32[]{:S(2)}, u32[]{:S(2)}) async-start(bf16[8,3,256,128]{3,2,1,0:T(8,128)(2,1)} %get-tuple-element.327), calls=%async_computation.7 | async-start | bytes 3145728 | tf_op jit(solution)/shard_map/cond/branch_1_fun/all_to_all | solution.py:42
  134.2 29.9 %all-to-all-start = ((bf16[8,2,256,128]{3,2,1,0:T(8,128)(2,1)}), bf16[8,2,256,128]{3,2,1,0:T(8,128)(2,1)}, u32[]{:S(2)}, u32[]{:S(2)}) async-start(bf16[8,2,256,128]{3,2,1,0:T(8,128)(2,1)} %get-tuple-element.336), calls=%async_computation | async-start | bytes 2097152 | tf_op jit(solution)/shard_map/cond/branch_1_fun/all_to_all | solution.py:42
  164.1 21.8 %all-to-all-start.1 = ((bf16[8,1,256,128]{3,2,1,0:T(8,128)(2,1)}), bf16[8,1,256,128]{3,2,1,0:T(8,128)(2,1)}, u32[]{:S(2)}, u32[]{:S(2)}) async-start(bf16[8,1,256,128]{3,2,1,0:T(8,128)(2,1)} %get-tuple-element.343), calls=%async_computation.1 | async-start | bytes 1048576 | tf_op jit(solution)/shard_map/cond/branch_1_fun/all_to_all | solution.py:42
  186.1 33.6 %all-to-all-start.2 = ((bf16[8,1,256,128]{3,2,1,0:T(8,128)(2,1)}), bf16[8,1,256,128]{3,2,1,0:T(8,128)(2,1)}, u32[]{:S(2)}, u32[]{:S(2)}) async-start(bf16[8,1,256,128]{3,2,1,0:T(8,128)(2,1)} %get-tuple-element.366), calls=%async_computation.2 | async-start | bytes 1048576 | tf_op jit(solution)/shard_map/cond/branch_1_fun/all_to_all | solution.py:42
  231.1 52.0 %collective-permute-start.24 = (bf16[8,128,1024]{2,1,0:T(8,128)(2,1)}, bf16[8,128,1024]{2,1,0:T(8,128)(2,1)}, u32[]{:S(2)}, u32[]{:S(2)}) collective-permute-start(bf16[8,128,1024]{2,1,0:T(8,128)(2,1)} %weight_part.31), channel_id=1, source_target_pairs={{0,8},{8,0},{16,24},{24,16},{1,9},{9,1},{17,25},{25,17},{2,10},{10... | collective-permute-start | bytes 6291464 | tf_op jit(solution)/shard_map/ppermute | solution.py:614
  237.8 47.9 %collective-permute-start.26 = (bf16[8,128,1024]{2,1,0:T(8,128)(2,1)}, bf16[8,128,1024]{2,1,0:T(8,128)(2,1)}, u32[]{:S(2)}, u32[]{:S(2)}) collective-permute-start(bf16[8,128,1024]{2,1,0:T(8,128)(2,1)} %weight_part.32), channel_id=1, source_target_pairs={{0,16},{8,24},{16,0},{24,8},{1,17},{9,25},{17,1},{25,9},{2,18},{10... | collective-permute-start | bytes 6291464 | tf_op jit(solution)/shard_map/ppermute | solution.py:614
  244.5 31.9 %collective-permute-start.20 = (bf16[8,128,1024]{2,1,0:T(8,128)(2,1)}, bf16[8,128,1024]{2,1,0:T(8,128)(2,1)}, u32[]{:S(2)}, u32[]{:S(2)}) collective-permute-start(bf16[8,128,1024]{2,1,0:T(8,128)(2,1)} %weight_part.19), channel_id=1, source_target_pairs={{0,8},{8,0},{16,24},{24,16},{1,9},{9,1},{17,25},{25,17},{2,10},{10... | collective-permute-start | bytes 6291464 | tf_op jit(solution)/shard_map/cond/branch_1_fun/ppermute | solution.py:614
  244.5 38.1 %all-to-all-start.4 = ((bf16[8,2,256,128]{3,2,1,0:T(8,128)(2,1)}), bf16[8,2,256,128]{3,2,1,0:T(8,128)(2,1)}, u32[]{:S(2)}, u32[]{:S(2)}) async-start(bf16[8,2,256,128]{3,2,1,0:T(8,128)(2,1)} %get-tuple-element.390), calls=%async_computation.4 | async-start | bytes 2097152 | tf_op jit(solution)/shard_map/cond/branch_1_fun/all_to_all | solution.py:42
  282.6 53.1 %collective-permute-start.28 = (bf16[8,128,1024]{2,1,0:T(8,128)(2,1)}, bf16[8,128,1024]{2,1,0:T(8,128)(2,1)}, u32[]{:S(2)}, u32[]{:S(2)}) collective-permute-start(bf16[8,128,1024]{2,1,0:T(8,128)(2,1)} %get-tuple-element.738), channel_id=1, source_target_pairs={{0,16},{8,24},{16,0},{24,8},{1,17},{9,25},{17,1},{25,9},{2,18},{10... | collective-permute-start | bytes 6291464 | tf_op jit(solution)/shard_map/ppermute | solution.py:614
  285.7 44.6 %all-to-all-start.5 = ((bf16[8,1,3,256,128]{4,3,2,1,0:T(8,128)(2,1)}), bf16[8,1,3,256,128]{4,3,2,1,0:T(8,128)(2,1)}, u32[]{:S(2)}, u32[]{:S(2)}) async-start(bf16[8,1,3,256,128]{4,3,2,1,0:T(8,128)(2,1)} %get-tuple-element.408), calls=%async_computation.5 | async-start | bytes 3145728 | tf_op jit(solution)/shard_map/cond/branch_1_fun/all_to_all | solution.py:42
  333.6 46.4 %collective-permute-start.30 = (bf16[4,128,1024]{2,1,0:T(8,128)(2,1)S(1)}, bf16[4,128,1024]{2,1,0:T(8,128)(2,1)}, u32[]{:S(2)}, u32[]{:S(2)}) collective-permute-start(bf16[4,128,1024]{2,1,0:T(8,128)(2,1)S(1)} %get-tuple-element.734), channel_id=1, source_target_pairs={{0,1},{1,0},{2,3},{3,2},{4,5},{5,4},{6,7},{7,6},{8,9},{9,8},{10,11... | collective-permute-start | bytes 3145736 | tf_op jit(solution)/shard_map/ppermute | solution.py:614
  336.4 43.5 %all-to-all-start.6 = ((bf16[8,1,3,256,128]{4,3,2,1,0:T(8,128)(2,1)}), bf16[8,1,3,256,128]{4,3,2,1,0:T(8,128)(2,1)}, u32[]{:S(2)}, u32[]{:S(2)}) async-start(bf16[8,1,3,256,128]{4,3,2,1,0:T(8,128)(2,1)} %get-tuple-element.437), calls=%async_computation.6 | async-start | bytes 3145728 | tf_op jit(solution)/shard_map/cond/branch_1_fun/all_to_all | solution.py:42
  383.5 42.3 %collective-permute-start.32 = (bf16[4,128,1024]{2,1,0:T(8,128)(2,1)}, bf16[4,128,1024]{2,1,0:T(8,128)(2,1)}, u32[]{:S(2)}, u32[]{:S(2)}) collective-permute-start(bf16[4,128,1024]{2,1,0:T(8,128)(2,1)} %get-tuple-element.744), channel_id=1, source_target_pairs={{0,1},{1,0},{2,3},{3,2},{4,5},{5,4},{6,7},{7,6},{8,9},{9,8},{10,11... | collective-permute-start | bytes 3145736 | tf_op jit(solution)/shard_map/ppermute | solution.py:614
  385.0 40.8 %collective-permute-start.31 = (bf16[2,128,1024]{2,1,0:T(8,128)(2,1)S(1)}, bf16[2,128,1024]{2,1,0:T(8,128)(2,1)S(1)}, u32[]{:S(2)}, u32[]{:S(2)}) collective-permute-start(bf16[2,128,1024]{2,1,0:T(8,128)(2,1)S(1)} %get-tuple-element.743), channel_id=1, source_target_pairs={{0,2},{1,3},{2,0},{3,1},{4,6},{5,7},{6,4},{7,5},{8,10},{9,11},{10,... | collective-permute-start | bytes 1572872 | tf_op jit(solution)/shard_map/ppermute | solution.py:614
  385.0 40.8 %all-to-all-start.3 = ((bf16[8,1,3,256,128]{4,3,2,1,0:T(8,128)(2,1)}), bf16[8,1,3,256,128]{4,3,2,1,0:T(8,128)(2,1)}, u32[]{:S(2)}, u32[]{:S(2)}) async-start(bf16[8,1,3,256,128]{4,3,2,1,0:T(8,128)(2,1)} %get-tuple-element.462), calls=%async_computation.3 | async-start | bytes 3145728 | tf_op jit(solution)/shard_map/cond/branch_1_fun/all_to_all | solution.py:42
  451.7 25.5 %collective-permute-start.2 = (bf16[4,128,1024]{2,1,0:T(8,128)(2,1)}, bf16[4,128,1024]{2,1,0:T(8,128)(2,1)}, u32[]{:S(2)}, u32[]{:S(2)}) collective-permute-start(bf16[4,128,1024]{2,1,0:T(8,128)(2,1)} %get-tuple-element.485), channel_id=1, source_target_pairs={{0,1},{1,0},{2,3},{3,2},{4,5},{5,4},{6,7},{7,6},{8,9},{9,8},{10,11... | collective-permute-start | bytes 3145736 | tf_op jit(solution)/shard_map/cond/branch_1_fun/ppermute | solution.py:614
  453.2 24.9 %collective-permute-start.3 = (bf16[8,128,512]{2,1,0:T(8,128)(2,1)S(1)}, bf16[8,128,512]{2,1,0:T(8,128)(2,1)}, u32[]{:S(2)}, u32[]{:S(2)}) collective-permute-start(bf16[8,128,512]{2,1,0:T(8,128)(2,1)S(1)} %get-tuple-element.486), channel_id=1, source_target_pairs={{0,16},{8,24},{16,0},{24,8},{1,17},{9,25},{17,1},{25,9},{2,18},{10... | collective-permute-start | bytes 3145736 | tf_op jit(solution)/shard_map/cond/branch_1_fun/ppermute | solution.py:614
  453.2 19.3 %collective-permute-start.1 = (bf16[2,128,1024]{2,1,0:T(8,128)(2,1)S(1)}, bf16[2,128,1024]{2,1,0:T(8,128)(2,1)}, u32[]{:S(2)}, u32[]{:S(2)}) collective-permute-start(bf16[2,128,1024]{2,1,0:T(8,128)(2,1)S(1)} %get-tuple-element.484), channel_id=1, source_target_pairs={{0,2},{1,3},{2,0},{3,1},{4,6},{5,7},{6,4},{7,5},{8,10},{9,11},{10,... | collective-permute-start | bytes 1572872 | tf_op jit(solution)/shard_map/cond/branch_1_fun/ppermute | solution.py:614
  453.3 17.1 %collective-permute-start = (bf16[1,128,1024]{2,1,0:T(8,128)(2,1)}, bf16[1,128,1024]{2,1,0:T(8,128)(2,1)}, u32[]{:S(2)}, u32[]{:S(2)}) collective-permute-start(bf16[1,128,1024]{2,1,0:T(8,128)(2,1)} %get-tuple-element.483), channel_id=1, source_target_pairs={{0,4},{1,5},{2,6},{3,7},{4,0},{5,1},{6,2},{7,3},{8,12},{9,13},{10,... | collective-permute-start | bytes 786440 | tf_op jit(solution)/shard_map/cond/branch_1_fun/ppermute | solution.py:614
  484.5 16.7 %collective-permute-start.4 = (bf16[4,128,512]{2,1,0:T(8,128)(2,1)S(1)}, bf16[4,128,512]{2,1,0:T(8,128)(2,1)}, u32[]{:S(2)}, u32[]{:S(2)}) collective-permute-start(bf16[4,128,512]{2,1,0:T(8,128)(2,1)S(1)} %get-tuple-element.503), channel_id=1, source_target_pairs={{0,1},{1,0},{2,3},{3,2},{4,5},{5,4},{6,7},{7,6},{8,9},{9,8},{10,11... | collective-permute-start | bytes 1572872 | tf_op jit(solution)/shard_map/cond/branch_1_fun/ppermute | solution.py:614
  485.2 18.4 %collective-permute-start.5 = (bf16[2,128,1024]{2,1,0:T(8,128)(2,1)S(1)}, bf16[2,128,1024]{2,1,0:T(8,128)(2,1)}, u32[]{:S(2)}, u32[]{:S(2)}) collective-permute-start(bf16[2,128,1024]{2,1,0:T(8,128)(2,1)S(1)} %get-tuple-element.504), channel_id=1, source_target_pairs={{0,2},{1,3},{2,0},{3,1},{4,6},{5,7},{6,4},{7,5},{8,10},{9,11},{10,... | collective-permute-start | bytes 1572872 | tf_op jit(solution)/shard_map/cond/branch_1_fun/ppermute | solution.py:614
  485.2 16.1 %collective-permute-start.6 = (bf16[1,128,1024]{2,1,0:T(8,128)(2,1)S(1)}, bf16[1,128,1024]{2,1,0:T(8,128)(2,1)}, u32[]{:S(2)}, u32[]{:S(2)}) collective-permute-start(bf16[1,128,1024]{2,1,0:T(8,128)(2,1)S(1)} %get-tuple-element.505), channel_id=1, source_target_pairs={{0,4},{1,5},{2,6},{3,7},{4,0},{5,1},{6,2},{7,3},{8,12},{9,13},{10,... | collective-permute-start | bytes 786440 | tf_op jit(solution)/shard_map/cond/branch_1_fun/ppermute | solution.py:614
  (56 other events, 523.0 us)
where the time goes:
time: 560 us; the launch traced here: 549 us
  Pallas kernels  327 us (58%)
  waiting for transfers between devices  113 us (20%)
  starting transfers between devices  77.5 us (14%)
  matrix products  12.6 us (2%)
  local copies, waits for them, and re-layouts  7.4 us (1%)
  loops' own time  7.29 us (1%)
    pallas_call x19, Pallas kernels, weight_part(): pl.pallas_call(functools.partial(weight_kernel, len(pairs), len(pairs[0][...  95.2 us
    pallas_call x3, Pallas kernels, attend_back(): pl.pallas_call(functools.partial(attend_back_kernel, slot, heads, head_di...  67 us
    all_to_all x10, waiting for transfers between devices, exchange(): return lax.all_to_all(parts, 'blk', 0, 0, tiled=True)  59 us
    ppermute x35, waiting for transfers between devices, flip(): return lax.ppermute(value, axis, [(i, i ^ 1 << bit) for i in range(size)])  53.9 us
    all_to_all x10, starting transfers between devices, exchange(): return lax.all_to_all(parts, 'blk', 0, 0, tiled=True)  53.4 us
    pallas_call x3, Pallas kernels, attend(): pl.pallas_call(functools.partial(attend_kernel, slot, heads, head_dim), g...  51.4 us
    pallas_call x2, Pallas kernels, layer(): pl.pallas_call(functools.partial(layer_kernel, slots), grid_spec=pltpu.Pr...  44.8 us
    ppermute x35, starting transfers between devices, flip(): return lax.ppermute(value, axis, [(i, i ^ 1 << bit) for i in range(size)])  24.1 us
  transfers between devices with their start and end apart: 45, of which 22 were waited for; matrix products, arithmetic and copies ran while one was open for 3% of the time, Pallas kernels for 52%

commit v1 on v0

--- a/solution.py
+++ b/solution.py
@@ -803,13 +803,15 @@
             continue
 
         def put(ref, j, i):
-            if kind == "add":
-                ref[j] = (terms[0][i].astype(F32) + terms[1][i].astype(F32)).astype(BF16)
-                return
-            at = 0
-            for term in terms:
-                ref[j, :, at : at + term.shape[2]] = term[i]
-                at += term.shape[2]
+            at, each = 0, 2 if kind == "add" else 1
+            for m in range(0, len(terms), each):
+                to = slice(at, at + terms[m].shape[2])
+                if kind == "add":
+                    total = terms[m][i].astype(F32) + terms[m + 1][i].astype(F32)
+                    ref[j, :, to] = total.astype(BF16)
+                else:
+                    ref[j, :, to] = terms[m][i]
+                at = to.stop
 
         if cut:
             keep, send = out_of.pop(0), out_of.pop(0)
@@ -854,8 +856,9 @@
         plan.append((state, len(tree.terms), cut))
         ins += tree.terms
         count, high, wide = tree.terms[0].shape
-        if state == "first":
-            wide = sum(term.shape[2] for term in tree.terms)
+        if state != "stack":
+            each = 1 if state == "first" else 2
+            wide = sum(term.shape[2] for term in tree.terms[::each])
         count = count // 2 if cut else 2 if state == "stack" else count
         shapes += [jax.ShapeDtypeStruct((count, high, wide), BF16)] * (2 if cut else 1)
         at.append((me >> bit) & 1 if cut else me * 0)
@@ -939,40 +942,84 @@
         self.terms = [self.kept, arrived]
 
 
-def input_grad_kernel(parts, order_ref, x_ref, gain_ref, wq_ref, wk_ref, wv_ref, *refs):
-    out_ref, sum_ref = refs[-2:]
-    rows, span, model = x_ref.shape
+def input_grad_kernel(slots, parts, order_ref, gain_ref, x_hbm, *refs):
+    wq_ref, wk_ref, wv_ref = refs[:3]
+    count = len(slots)
+    d_refs, value_refs, res_refs = refs[3 : 3 + count], refs[3 + count : 3 + 2 * count], refs[3 + 2 * count : -4]
+    out_ref, sum_ref, x_ref, sems = refs[-4:]
+    span, model = x_ref.shape[1:]
     piece = model // parts
+    copies = [
+        pltpu.make_async_copy(x_hbm.at[order_ref[slot]], x_ref.at[n], sems.at[n])
+        for n, slot in enumerate(slots)
+    ]
+    for copy in copies:
+        copy.start()
+    residuals = [held.at[pl.ds(at, span)] for held in res_refs for at in range(0, held.shape[0], span)]
+    residuals = residuals[-count:] if slots[0] else residuals[:count]
+    for copy in copies:
+        copy.wait()
     total = jnp.zeros(sum_ref.shape, F32)
-    residuals = [
-        held.at[pl.ds(at, span)] for held in refs[2 * rows : -2] for at in range(0, held.shape[0], span)
-    ]
-    for r in range(rows):
-        d_ref, value_ref, res_ref = refs[r], refs[rows + r], residuals[r]
-        grad = dot_last(value_ref[...], wv_ref[...])
+    for n in range(count):
+        grad = dot_last(value_refs[n][...], wv_ref[...])
         for p in range(parts):
-            for n, weight in enumerate((wq_ref, wk_ref)):
-                at = (p * 2 + n) * piece
-                grad += dot_last(d_ref[:, at : at + piece], weight[:, p * piece : (p + 1) * piece])
-        row = order_ref[r]
-        hat, spread = norm_parts(x_ref[row].astype(F32))
-        out_ref[row] = res_ref[...] + norm_back(hat, spread, gain_ref[...], grad)
+            for m, weight in enumerate((wq_ref, wk_ref)):
+                at = (p * 2 + m) * piece
+                grad += dot_last(d_refs[n][:, at : at + piece], weight[:, p * piece : (p + 1) * piece])
+        hat, spread = norm_parts(x_ref[n].astype(F32))
+        out_ref[n] = residuals[n][...] + norm_back(hat, spread, gain_ref[...], grad)
         total += jnp.sum(grad * hat, axis=0, keepdims=True)
     sum_ref[...] = total
 
 
-def input_grad(order, x, gain, w_query, w_key, w_value, d_rows, d_values, d_residuals):
+def input_grad(order, slots, x, gain, weights, d_rows, d_values, d_residuals):
+    _, span, model = x.shape
+    count = len(slots)
     return pl.pallas_call(
-        functools.partial(input_grad_kernel, PARTS),
-        in_specs=[SMEM] + [VMEM] * (5 + 2 * len(d_rows) + len(d_residuals)),
+        functools.partial(input_grad_kernel, slots, PARTS),
+        in_specs=[SMEM, VMEM, pl.BlockSpec(memory_space=pl.ANY)]
+        + [VMEM] * (3 + 2 * count + len(d_residuals)),
         out_shape=[
-            jax.ShapeDtypeStruct(x.shape, F32),
-            jax.ShapeDtypeStruct((1, x.shape[2]), F32),
+            jax.ShapeDtypeStruct((count, span, model), F32),
+            jax.ShapeDtypeStruct((1, model), F32),
+        ],
+        scratch_shapes=[
+            pltpu.VMEM((count, span, model), BF16),
+            pltpu.SemaphoreType.DMA((count,)),
         ],
         compiler_params=kernel_params(),
         cost_estimate=cost(0, 1024),
         name="input_grad",
-    )(order, x, gain, w_query, w_key, w_value, *d_rows, *d_values, *d_residuals)
+    )(order, gain, x, *weights, *d_rows, *d_values, *d_residuals)
+
+
+def in_place_kernel(order_ref, *refs):
+    *ins, out_ref, sems = refs
+    copies, slot = [], 0
+    for part in ins:
+        for n in range(part.shape[0]):
+            copies.append(
+                pltpu.make_async_copy(part.at[n], out_ref.at[order_ref[slot]], sems.at[slot])
+            )
+            slot += 1
+    for copy in copies:
+        copy.start()
+    for copy in copies:
+        copy.wait()
+
+
+def in_place(order, parts):
+    rows = order.shape[0]
+    return pl.pallas_call(
+        in_place_kernel,
+        in_specs=[SMEM] + [pl.BlockSpec(memory_space=pl.ANY)] * len(parts),
+        out_specs=pl.BlockSpec(memory_space=pl.ANY),
+        out_shape=jax.ShapeDtypeStruct((rows, *parts[0].shape[1:]), parts[0].dtype),
+        scratch_shapes=[pltpu.SemaphoreType.DMA((rows,))],
+        compiler_params=kernel_params(),
+        cost_estimate=cost(0, 1024),
+        name="in_place",
+    )(order, *parts)
 
 
 def on_device(
@@ -1165,26 +1212,37 @@
             mine_two, mine_three = out_of
     tree_one.end(moved)
     tree_two = Tree(mine_two)
-    combine([tree_one, tree_two])
-
+    tree_three = Tree(mine_three, halved=1)
+    combine([tree_one, tree_two, tree_three])
     moved = tree_one.start(), tree_two.start()
+    moved_three = tree_three.start()
     sent = tie(sent, tree_one.send, tree_two.send)
 
     def back_last():
         order = Order()
         grad = exchange(sent)
         joined = [order(join_grads, part) for part in grads]
-
-        def output_step(weight):
-            return last_step(by_work, inputs.shape, residual, mid, weight)
-
         d_rows, d_values = zip(*joined)
         early_qk = WeightSum((normed[:last], d_rows, "columns"))
         early_v = WeightSum((normed[:last], d_values, "columns"))
         early = [early_qk.away(order), early_v.away(order), early_qk.own(order), early_v.own(order)]
-        return grad, joined, order(output_step, w_fc2), early
-
-    grad, joined, layer_out, early_sums = window(always, back_last)
+        part = order(
+            lambda x: input_grad(
+                by_work,
+                list(rows[:last]),
+                x,
+                gain,
+                (w_query, w_key, w_value),
+                d_rows,
+                d_values,
+                d_residual,
+            ),
+            inputs,
+        )
+        return grad, joined, part, early
+
+    grad, joined, part, early_sums = window(always, back_last)
+    early_grads, early_gain = part
     early_away_qk, early_away_v, early_qk, early_v = early_sums
     grad, moved = tie((grad, moved))
     tree_one.end(moved[0])
@@ -1197,8 +1255,12 @@
     away_qk = over_near(sum_qk.away(order, (early_away_qk, sum_qk.zero)))
     away_v = over_near(sum_v.away(order, (early_away_v, sum_v.zero)))
     sent_qk = sum_qk.send(order, away_qk, early_qk)
-    tree_v = Tree(sum_v.own(order, away_v, early_v), mine_three, halved=1)
-    combine([tree_one, tree_two, tree_v])
+    far_qk = over_far(sent_qk)
+    for tree in (tree_one, tree_two):
+        tree.terms = list(tie(tree.terms, sent_qk))
+    combine([tree_one, tree_two])
+    moved = tree_one.start(), tree_two.start()
+    away_v = tie(away_v, tree_one.send, tree_two.send)
 
     def advance(trees, extra=lambda: ()):
         def step():
@@ -1211,18 +1273,32 @@
 
     def beside():
         order = Order()
-        arrived = over_far(sent_qk)
+        tree = Tree(sum_v.own(order, away_v, early_v), halved=1)
+        combine([tree])
 
         def input_step(x):
             return input_grad(
-                by_work, x, gain, w_query, w_key, w_value, d_rows, d_values, d_residual
+                by_work,
+                [last],
+                x,
+                gain,
+                (w_query, w_key, w_value),
+                d_rows[last:],
+                d_values[last:],
+                d_residual,
             )
 
-        return arrived, order(input_step, inputs)
-
-    far_qk, (grad_inputs, grad_ln_attn) = advance(
-        [tree_one, tree_two, tree_v], beside
-    )
+        return tree.kept, tree.start(), order(input_step, inputs)
+
+    kept, arrived, (late_grads, late_gain) = window(always, beside)
+    moved, arrived = tie((moved, arrived))
+    tree_one.end(moved[0])
+    tree_two.end(moved[1])
+    grad_ln_attn = early_gain + late_gain
+    tree_v = Tree(halved=1)
+    tree_v.kept = kept
+    tree_v.end(arrived)
+    tree_v.terms += [tree_three.kept, moved_three]
     tree_qk = Tree(sum_qk.keep_rest(order, far_qk, away_qk, early_qk))
     delta_sum = sum(jnp.sum(total, axis=1) for total in totals)
     my_grad = delta_sum[:heads] / my_scale
@@ -1237,19 +1313,33 @@
     piece = model // PARTS
     ff_piece = w_fc1.shape[1] // PARTS
     trees = [tree_qk, tree_v, tree_two, tree_one]
-    placed = None
+    placed = layer_out = grad_inputs = None
     while any(tree.steps for tree in trees + [small]):
         combine([tree for tree in trees + [small] if tree.steps])
 
-        def place_early():
+        def beside_step():
+            if layer_out is None:
+                order = Order()
+
+                def output_step(weight):
+                    return last_step(by_work, inputs.shape, residual, mid, weight)
+
+                return order(output_step, w_fc2)
+            if grad_inputs is None:
+                return in_place(by_work, [early_grads, late_grads])
             if tree_two.steps or tree_one.steps or placed is not None:
                 return ()
             return place(
                 [tree_one, tree_two], [[(0, model, "rows")], [(0, ff_piece, "columns")]]
             )
 
-        early_out = advance([tree for tree in trees + [small] if tree.steps], place_early)
-        placed = early_out or placed
+        beside_out = advance([tree for tree in trees + [small] if tree.steps], beside_step)
+        if layer_out is None:
+            layer_out = beside_out
+        elif grad_inputs is None:
+            grad_inputs = beside_out
+        else:
+            placed = beside_out or placed
     if placed is None:
         placed = place([tree_one, tree_two], [[(0, model, "rows")], [(0, ff_piece, "columns")]])
     grad_fc2, grad_fc1 = placed

time: 560 us -> 557 us (level)
  waiting for transfers between devices: 113 us -> 102 us
  starting transfers between devices: 77.5 us -> 84.6 us
    ppermute x35 -> x36, waiting for transfers between devices: 53.9 us -> 32 us  [flip(): return lax.ppermute(value, axis, [(i, i ^ 1 << bit) for i in range(size)])]
    all_to_all x10, waiting for transfers between devices: 59 us -> 69.8 us  [exchange(): return lax.all_to_all(parts, 'blk', 0, 0, tiled=True)]
    ppermute x35 -> x36, starting transfers between devices: 24.1 us -> 32.4 us  [flip(): return lax.ppermute(value, axis, [(i, i ^ 1 << bit) for i in range(size)])]
    pallas_call x1 -> x3, Pallas kernels: 11.6 us -> 18.1 us  [the longest x2 15.7 us: input_grad(): pl.pallas_call(functools.partial(input_grad_kernel, slots, PARTS), in_spe...]
    pallas_call x8 -> x9, Pallas kernels: 15.9 us -> 17.6 us  [combine(): pl.pallas_call(functools.partial(combine_kernel, plan), in_specs=[SMEM] +...]
  transfers between devices with their start and end apart: 45 -> 46, of which waited for: 22 -> 20; matrix products, arithmetic and copies ran while one was open for 3% -> 3% of each run, Pallas kernels for 52% -> 54%
where the time goes in v1:
time: 557 us; the launch traced here: 546 us
  Pallas kernels  329 us (59%)
  waiting for transfers between devices  102 us (18%)
  starting transfers between devices  84.6 us (15%)
  matrix products  12.6 us (2%)
  local copies, waits for them, and re-layouts  7.64 us (1%)
  loops' own time  7.45 us (1%)
    pallas_call x19, Pallas kernels, weight_part(): pl.pallas_call(functools.partial(weight_kernel, len(pairs), len(pairs[0][...  92.6 us
    all_to_all x10, waiting for transfers between devices, exchange(): return lax.all_to_all(parts, 'blk', 0, 0, tiled=True)  69.8 us
    pallas_call x3, Pallas kernels, attend_back(): pl.pallas_call(functools.partial(attend_back_kernel, slot, heads, head_di...  64.1 us
    all_to_all x10, starting transfers between devices, exchange(): return lax.all_to_all(parts, 'blk', 0, 0, tiled=True)  52.2 us
    pallas_call x3, Pallas kernels, attend(): pl.pallas_call(functools.partial(attend_kernel, slot, heads, head_dim), g...  50.7 us
    pallas_call x2, Pallas kernels, layer(): pl.pallas_call(functools.partial(layer_kernel, slots), grid_spec=pltpu.Pr...  45 us
    ppermute x36, starting transfers between devices, flip(): return lax.ppermute(value, axis, [(i, i ^ 1 << bit) for i in range(size)])  32.4 us
    ppermute x36, waiting for transfers between devices, flip(): return lax.ppermute(value, axis, [(i, i ^ 1 << bit) for i in range(size)])  32 us
  transfers between devices with their start and end apart: 46, of which 20 were waited for; matrix products, arithmetic and copies ran while one was open for 3% of the time, Pallas kernels for 54%

profile of v1, /device:TPU:0, one launch (start us, length us, event | category | flops | bytes accessed | tf_op | source)
XLA Modules:
  0.0 546.1 jit_solution(11236647007178564547)
XLA Ops:
  26.7 24.4 %all-to-all-done.9 = bf16[8,3,256,128]{3,2,1,0:T(8,128)(2,1)} async-done(((bf16[8,3,256,128]{3,2,1,0:T(8,128)(2,1)}), bf16[8,3,256,128]{3,2,1,0:T(8,128)(2,1)}, u32[]{:S(2)}, u32[]{:S(2)}) %all-to-all-start.9) | async-done | bytes 1572896 | tf_op jit(solution)/shard_map/all_to_all | solution.py:42
  51.0 41.1 %conditional.15 = (bf16[8,3,256,128]{3,2,1,0:T(8,128)(2,1)}, bf16[8,2,256,128]{3,2,1,0:T(8,128)(2,1)S(1)}, f32[8,2,256]{2,1,0:T(2,128)S(1)}, f32[768,4096]{1,0:T(8,128)}) conditional(s32[]{:T(128)} %bitcast.23, () %tuple.172, (bf16[8,3,256,128]{3,2,1,0:T(8,128)(2,1)}, s32[3]{0:T(128)S(1)}, s32[3,4]{1,0:T(4,128)S(1)}, f32[1,128]{1,0:T(1,128)S(1)}, ...), branch_computations={%region_0.0_spmd, %region_1.0_spmd} | conditional | flops 6442450944 | bytes 33555548 | solution.py:785
  55.5 19.4 %attend.3 = (bf16[8,2,256,128]{3,2,1,0:T(8,128)(2,1)S(1)}, f32[8,2,256]{2,1,0:T(2,128)S(1)}) custom-call(s32[3]{0:T(128)S(1)} %get-tuple-element.332.order_ref, s32[3,4]{1,0:T(4,128)S(1)} %get-tuple-element.333.offs_ref, f32[1,128]{1,0:T(1,128)S(1)} %get-tuple-element.334.scale_ref, bf16[8,3,256,128]{3,2,1,0:T(8,128)(2,1)} %get-tuple-element.335.held), custom_call_target="tpu_custom_call" | custom-call | bytes 1024 | tf_op jit(solution)/shard_map/cond/branch_1_fun/attend/pallas_call | solution.py:252
  74.9 12.6 %fusion.4 = f32[768,4096]{1,0:T(8,128)} fusion(bf16[768,1024]{1,0:T(8,128)(2,1)S(1)} %bitcast.56, bf16[4096,1024]{1,0:T(8,128)(2,1)} %get-tuple-element.339), kind=kOutput, calls=%fused_computation.32 | convolution fusion | flops 6442450944 | bytes 22544384 | tf_op jit(solution)/shard_map/cond/branch_1_fun/td,fd->tf/dot_general | solution.py:1108
  92.1 41.1 %conditional.16 = (bf16[8,3,256,128]{3,2,1,0:T(8,128)(2,1)}, bf16[8,2,256,128]{3,2,1,0:T(8,128)(2,1)}, f32[8,2,256]{2,1,0:T(2,128)S(1)}, bf16[256,1024]{1,0:T(8,128)(2,1)S(1)}, bf16[512,1024]{1,0:T(8,128)(2,1)S(1)}) conditional(s32[]{:T(128)} %bitcast.23, () %tuple.170, (bf16[8,3,256,128]{3,2,1,0:T(8,128)(2,1)}, s32[3]{0:T(128)S(1)}, ...), branch_computations={%region_2.0_spmd, %region_3.4_spmd} | conditional | flops 2097161 | bytes 18351342 | solution.py:785
  100.9 16.7 %attend.4 = (bf16[8,2,256,128]{3,2,1,0:T(8,128)(2,1)S(1)}, f32[8,2,256]{2,1,0:T(2,128)S(1)}) custom-call(s32[3]{0:T(128)S(1)} %get-tuple-element.341.order_ref, s32[3,4]{1,0:T(4,128)S(1)} %get-tuple-element.342.offs_ref, f32[1,128]{1,0:T(1,128)S(1)} %get-tuple-element.343.scale_ref, ...), custom_call_target="tpu_custom_call", output_to_operand_aliasing={{0}: (4, {})} | custom-call | bytes 1024 | tf_op jit(solution)/shard_map/cond/branch_1_fun/attend/pallas_call | solution.py:252
  120.8 12.2 %all-to-all-done.7 = bf16[8,3,256,128]{3,2,1,0:T(8,128)(2,1)} async-done(((bf16[8,3,256,128]{3,2,1,0:T(8,128)(2,1)}), bf16[8,3,256,128]{3,2,1,0:T(8,128)(2,1)}, u32[]{:S(2)}, u32[]{:S(2)}) %all-to-all-start.7) | async-done | bytes 1572896 | tf_op jit(solution)/shard_map/cond/branch_1_fun/all_to_all | solution.py:42
  134.4 30.0 %conditional.17 = (bf16[8,2,256,128]{3,2,1,0:T(8,128)(2,1)}, bf16[8,1,256,128]{3,2,1,0:T(8,128)(2,1)}, f32[8,2,256]{2,1,0:T(2,128)S(1)}) conditional(s32[]{:T(128)} %bitcast.23, () %tuple.169, (bf16[8,2,256,128]{3,2,1,0:T(8,128)(2,1)}, s32[3]{0:T(128)S(1)}, s32[3,4]{1,0:T(4,128)S(1)}, f32[1,128]{1,0:T(1,128)S(1)}, ...), branch_computations={%region_4.5_spmd, %region_5.6_spmd} | conditional | bytes 3146808 | solution.py:785
  138.8 14.6 %attend.5 = (bf16[8,1,256,128]{3,2,1,0:T(8,128)(2,1)}, f32[8,2,256]{2,1,0:T(2,128)S(1)}) custom-call(s32[3]{0:T(128)S(1)} %get-tuple-element.350.order_ref, s32[3,4]{1,0:T(4,128)S(1)} %get-tuple-element.351.offs_ref, f32[1,128]{1,0:T(1,128)S(1)} %get-tuple-element.352.scale_ref, bf16[8,3,256,128]{3,2,1,0:T(8,128)(2,1)} %get-tuple-element.353.held), custom_call_target="tpu_custom_call" | custom-call | bytes 1024 | tf_op jit(solution)/shard_map/cond/branch_1_fun/attend/pallas_call | solution.py:252
  164.4 21.8 %conditional.18 = (bf16[8,1,256,128]{3,2,1,0:T(8,128)(2,1)}, bf16[256,1024]{1,0:T(8,128)(2,1)}, bf16[256,1024]{1,0:T(8,128)(2,1)}, f32[256,1024]{1,0:T(8,128)}, ...) conditional(s32[]{:T(128)} %bitcast.23, () %tuple.168, ...), branch_computations={%region_6.7_spmd, %region_7.8_spmd} | conditional | bytes 8937602 | solution.py:785
  169.0 17.1 %layer.2 = (bf16[256,1024]{1,0:T(8,128)(2,1)}, bf16[256,1024]{1,0:T(8,128)(2,1)}, f32[256,1024]{1,0:T(8,128)}, bf16[256,4096]{1,0:T(8,128)(2,1)}, bf16[256,4096]...) custom-call(s32[3]{0:T(128)S(1)} %get-tuple-element.357.order_ref, ...), custom_call_target="tpu_custom_call" | custom-call | bytes 1024 | tf_op jit(solution)/shard_map/cond/branch_1_fun/layer/pallas_call | solution.py:551
  186.3 34.3 %conditional.19 = (bf16[8,1,256,128]{3,2,1,0:T(8,128)(2,1)}, bf16[512,1024]{1,0:T(8,128)(2,1)}, bf16[512,1024]{1,0:T(8,128)(2,1)S(1)}, f32[512,1024]{1,0:T(8,128...) conditional(s32[]{:T(128)} %bitcast.23, () %tuple.167, ...), branch_computations={%region_8.9_spmd, %region_9.10_spmd} | conditional | bytes 17326210 | solution.py:785
  192.3 27.9 %layer.3 = (bf16[512,1024]{1,0:T(8,128)(2,1)}, bf16[512,1024]{1,0:T(8,128)(2,1)S(1)}, f32[512,1024]{1,0:T(8,128)}, bf16[512,4096]{1,0:T(8,128)(2,1)}, bf16[512,4...) custom-call(s32[3]{0:T(128)S(1)} %get-tuple-element.380.order_ref, ...), custom_call_target="tpu_custom_call" | custom-call | bytes 1024 | tf_op jit(solution)/shard_map/cond/branch_1_fun/layer/pallas_call | solution.py:551
  239.1 43.4 %conditional.20 = (bf16[8,2,256,128]{3,2,1,0:T(8,128)(2,1)}, bf16[8,1,3,256,128]{4,3,2,1,0:T(8,128)(2,1)}, bf16[8,128,1024]{2,1,0:T(8,128)(2,1)}, f32[8]{0:T(128)S(1)}) conditional(s32[]{:T(128)} %bitcast.23, () %tuple.166, (bf16[8,2,256,128]{3,2,1,0:T(8,128)(2,1)}, f32[1,128]{1,0:T(1,128)S(1)}, s32[]{:T(128)}, s32[]{:T(128)}, ...), branch_computations={%region_10.11_spmd, %region_11.0_spmd} | conditional | flops 2176 | bytes 11546852 | solution.py:785
  250.3 25.7 %attend_back.3 = (bf16[8,1,3,256,128]{4,3,2,1,0:T(8,128)(2,1)}, f32[8,256]{1,0:T(8,128)S(1)}) custom-call(s32[3]{0:T(128)S(1)} %get-tuple-element.404.order_ref, s32[3,4]{1,0:T(4,128)S(1)} %get-tuple-element.405.offs_ref, f32[1,128]{1,0:T(1,128)S(1)} %broadcast_divide_fusion.refs_0_, f32[8,2,256]{2,1,0:T(2,128)S(1)} %get-tuple-element.407.refs_1_, ...), custom_call_target="tpu_custom_call" | custom-call | bytes 1024 | tf_op jit(solution)/shard_map/cond/branch_1_fun/attend_back/pallas_call | solution.py:366
  285.4 42.4 %conditional.21 = (bf16[8,1,3,256,128]{4,3,2,1,0:T(8,128)(2,1)}, bf16[8,1,3,256,128]{4,3,2,1,0:T(8,128)(2,1)}, bf16[8,128,1024]{2,1,0:T(8,128)(2,1)}, bf16[8,128...) conditional(s32[]{:T(128)} %bitcast.23, () %tuple.165, ...), branch_computations={%region_13.14_spmd, %region_14.0_spmd} | conditional | flops 2173 | bytes 13120792 | solution.py:785
  291.4 18.8 %attend_back.4 = (bf16[8,1,3,256,128]{4,3,2,1,0:T(8,128)(2,1)}, f32[8,256]{1,0:T(8,128)S(1)}) custom-call(s32[3]{0:T(128)S(1)} %get-tuple-element.422.order_ref, s32[3,4]{1,0:T(4,128)S(1)} %get-tuple-element.423.offs_ref, f32[1,128]{1,0:T(1,128)S(1)} %broadcast_divide_fusion.1.refs_0_, f32[8,2,256]{2,1,0:T(2,128)S(1)} %get-tuple-element.425.refs_1_, ...), custom_call_target="tpu_custom_call" | custom-call | bytes 1024 | tf_op jit(solution)/shard_map/cond/branch_1_fun/attend_back/pallas_call | solution.py:366
  333.9 42.5 %conditional.22 = (bf16[8,1,3,256,128]{4,3,2,1,0:T(8,128)(2,1)}, bf16[8,128,1024]{2,1,0:T(8,128)(2,1)}, bf16[8,128,512]{2,1,0:T(8,128)(2,1)}, bf16[8,1,3,256,128]{4,3,2,1,0:T(8,128)(2,1)}, f32[8]{0:T(128)S(1)}) conditional(s32[]{:T(128)} %bitcast.23, () %tuple.164, (bf16[8,1,3,256,128]{4,3,2,1,0:T(8,128)(2,1)}, s32[]{:T(128)}, s32[]{:T(128)}, ...), branch_computations={%region_16.17_spmd, %region_17.0_spmd} | conditional | flops 2172 | bytes 6291540 | solution.py:785
  338.8 19.7 %attend_back.5 = (bf16[8,1,3,256,128]{4,3,2,1,0:T(8,128)(2,1)}, f32[8,256]{1,0:T(8,128)S(1)}) custom-call(s32[3]{0:T(128)S(1)} %get-tuple-element.453.order_ref, s32[3,4]{1,0:T(4,128)S(1)} %get-tuple-element.454.offs_ref, f32[1,128]{1,0:T(1,128)S(1)} %broadcast_divide_fusion.2.refs_0_, f32[8,2,256]{2,1,0:T(2,128)S(1)} %get-tuple-element.456.refs_1_, ...), custom_call_target="tpu_custom_call" | custom-call | bytes 1024 | tf_op jit(solution)/shard_map/cond/branch_1_fun/attend_back/pallas_call | solution.py:366
  381.9 40.8 %conditional.23 = (bf16[8,1,3,256,128]{4,3,2,1,0:T(8,128)(2,1)}, f32[2,256,1024]{2,1,0:T(8,128)}, f32[1,1024]{1,0:T(1,128)S(1)}, bf16[8,128,1024]{2,1,0:T(8,128)...) conditional(s32[]{:T(128)} %bitcast.23, () %tuple.163, ...), branch_computations={%region_19.20_spmd, %region_20.21_spmd} | conditional | flops 5 | bytes 34086172 | solution.py:785
  453.0 18.0 %conditional.24 = (bf16[4,128,512]{2,1,0:T(8,128)(2,1)}, bf16[4,128,512]{2,1,0:T(8,128)(2,1)}, f32[1,256,1024]{2,1,0:T(8,128)}, f32[1,1024]{1,0:T(1,128)S(1)}) conditional(s32[]{:T(128)} %bitcast.23, () %tuple.191, (s32[]{:T(128)}, bf16[256,1024]{1,0:T(8,128)(2,1)}, bf16[256,1024]{1,0:T(8,128)(2,1)}, bf16[8,128,512]{2,1,0:T(8,128)(2,1)}, ...), branch_computations={%region_21.22_spmd, %region_22.23_spmd} | conditional | flops 4 | bytes 25169144 | solution.py:785
  479.7 19.2 %conditional.25 = (bf16[4,128,512]{2,1,0:T(8,128)(2,1)}, bf16[2,128,1024]{2,1,0:T(8,128)(2,1)}, bf16[1,128,1024]{2,1,0:T(8,128)(2,1)}, bf16[1,128,1024]{2,1,0:T(...) conditional(s32[]{:T(128)} %bitcast.23, () %tuple.162, (bf16[4,128,512]{2,1,0:T(8,128)(2,1)S(1)}, ...), branch_computations={%region_23.24_spmd, %region_24.25_spmd} | conditional | bytes 6407672 | solution.py:785
  484.9 12.8 %layer_out.1 = bf16[3,256,1024]{2,1,0:T(8,128)(2,1)S(1)} custom-call(s32[3]{0:T(128)S(1)} %get-tuple-element.524.order_ref, f32[256,1024]{1,0:T(8,128)} %get-tuple-element.525.refs_0_, f32[512,1024]{1,0:T(8,128)} %get-tuple-element.526.refs_1_, bf16[256,4096]{1,0:T(8,128)(2,1)} %get-tuple-element.527.refs_2_, bf16[512,4096]{1,0:T(8,128)(2,1)} %get-tuple-element.528.refs_3_, ...), custom_call_target="tpu_custom_call" | custom-call | bytes 1024 | tf_op jit(solution)/shard_map/cond/branch_1_fun/layer_out/pallas_call | solution.py:602
  501.9 16.2 %conditional.26 = (bf16[2,128,512]{2,1,0:T(8,128)(2,1)}, bf16[1,128,1024]{2,1,0:T(8,128)(2,1)}, bf16[1,128,1024]{2,1,0:T(8,128)(2,1)}, bf16[2,128,1024]{2,1,0:T(...) conditional(s32[]{:T(128)} %bitcast.23, () %tuple.198, (bf16[2,128,512]{2,1,0:T(8,128)(2,1)S(1)}, ...), branch_computations={%region_25.26_spmd, %region_26.27_spmd} | conditional | bytes 5359096 | solution.py:785
  (273 shorter events, 336.2 us)
Async XLA Ops:
  6.5 44.5 %all-to-all-start.9 = ((bf16[8,3,256,128]{3,2,1,0:T(8,128)(2,1)}), bf16[8,3,256,128]{3,2,1,0:T(8,128)(2,1)}, u32[]{:S(2)}, u32[]{:S(2)}) async-start(bf16[8,3,256,128]{3,2,1,0:T(8,128)(2,1)} %get-tuple-element.731), calls=%async_computation.9 | async-start | bytes 3145728 | tf_op jit(solution)/shard_map/all_to_all | solution.py:42
  51.0 41.1 %all-to-all-start.8 = ((bf16[8,3,256,128]{3,2,1,0:T(8,128)(2,1)}), bf16[8,3,256,128]{3,2,1,0:T(8,128)(2,1)}, u32[]{:S(2)}, u32[]{:S(2)}) async-start(bf16[8,3,256,128]{3,2,1,0:T(8,128)(2,1)} %get-tuple-element.329), calls=%async_computation.8 | async-start | bytes 3145728 | tf_op jit(solution)/shard_map/cond/branch_1_fun/all_to_all | solution.py:42
  92.1 40.9 %all-to-all-start.7 = ((bf16[8,3,256,128]{3,2,1,0:T(8,128)(2,1)}), bf16[8,3,256,128]{3,2,1,0:T(8,128)(2,1)}, u32[]{:S(2)}, u32[]{:S(2)}) async-start(bf16[8,3,256,128]{3,2,1,0:T(8,128)(2,1)} %get-tuple-element.340), calls=%async_computation.7 | async-start | bytes 3145728 | tf_op jit(solution)/shard_map/cond/branch_1_fun/all_to_all | solution.py:42
  134.4 30.0 %all-to-all-start = ((bf16[8,2,256,128]{3,2,1,0:T(8,128)(2,1)}), bf16[8,2,256,128]{3,2,1,0:T(8,128)(2,1)}, u32[]{:S(2)}, u32[]{:S(2)}) async-start(bf16[8,2,256,128]{3,2,1,0:T(8,128)(2,1)} %get-tuple-element.349), calls=%async_computation | async-start | bytes 2097152 | tf_op jit(solution)/shard_map/cond/branch_1_fun/all_to_all | solution.py:42
  164.5 21.7 %all-to-all-start.1 = ((bf16[8,1,256,128]{3,2,1,0:T(8,128)(2,1)}), bf16[8,1,256,128]{3,2,1,0:T(8,128)(2,1)}, u32[]{:S(2)}, u32[]{:S(2)}) async-start(bf16[8,1,256,128]{3,2,1,0:T(8,128)(2,1)} %get-tuple-element.356), calls=%async_computation.1 | async-start | bytes 1048576 | tf_op jit(solution)/shard_map/cond/branch_1_fun/all_to_all | solution.py:42
  186.3 33.9 %all-to-all-start.2 = ((bf16[8,1,256,128]{3,2,1,0:T(8,128)(2,1)}), bf16[8,1,256,128]{3,2,1,0:T(8,128)(2,1)}, u32[]{:S(2)}, u32[]{:S(2)}) async-start(bf16[8,1,256,128]{3,2,1,0:T(8,128)(2,1)} %get-tuple-element.379), calls=%async_computation.2 | async-start | bytes 1048576 | tf_op jit(solution)/shard_map/cond/branch_1_fun/all_to_all | solution.py:42
  230.9 52.1 %collective-permute-start.21 = (bf16[8,128,1024]{2,1,0:T(8,128)(2,1)S(1)}, bf16[8,128,1024]{2,1,0:T(8,128)(2,1)}, u32[]{:S(2)}, u32[]{:S(2)}) collective-permute-start(bf16[8,128,1024]{2,1,0:T(8,128)(2,1)S(1)} %weight_part.32), channel_id=1, source_target_pairs={{0,8},{8,0},{16,24},{24,16},{1,9},{9,1},{17,25},{25,17},{2,10},{10... | collective-permute-start | bytes 6291464 | tf_op jit(solution)/shard_map/ppermute | solution.py:614
  237.5 47.9 %collective-permute-start.23 = (bf16[8,128,1024]{2,1,0:T(8,128)(2,1)}, bf16[8,128,1024]{2,1,0:T(8,128)(2,1)}, u32[]{:S(2)}, u32[]{:S(2)}) collective-permute-start(bf16[8,128,1024]{2,1,0:T(8,128)(2,1)} %weight_part.33), channel_id=1, source_target_pairs={{0,16},{8,24},{16,0},{24,8},{1,17},{9,25},{17,1},{25,9},{2,18},{10... | collective-permute-start | bytes 6291464 | tf_op jit(solution)/shard_map/ppermute | solution.py:614
  244.4 31.9 %collective-permute-start.17 = (bf16[8,128,1024]{2,1,0:T(8,128)(2,1)}, bf16[8,128,1024]{2,1,0:T(8,128)(2,1)}, u32[]{:S(2)}, u32[]{:S(2)}) collective-permute-start(bf16[8,128,1024]{2,1,0:T(8,128)(2,1)} %weight_part.19), channel_id=1, source_target_pairs={{0,8},{8,0},{16,24},{24,16},{1,9},{9,1},{17,25},{25,17},{2,10},{10... | collective-permute-start | bytes 6291464 | tf_op jit(solution)/shard_map/cond/branch_1_fun/ppermute | solution.py:614
  244.4 38.2 %all-to-all-start.4 = ((bf16[8,2,256,128]{3,2,1,0:T(8,128)(2,1)}), bf16[8,2,256,128]{3,2,1,0:T(8,128)(2,1)}, u32[]{:S(2)}, u32[]{:S(2)}) async-start(bf16[8,2,256,128]{3,2,1,0:T(8,128)(2,1)} %get-tuple-element.403), calls=%async_computation.4 | async-start | bytes 2097152 | tf_op jit(solution)/shard_map/cond/branch_1_fun/all_to_all | solution.py:42
  282.5 50.1 %collective-permute-start.25 = (bf16[8,128,1024]{2,1,0:T(8,128)(2,1)}, bf16[8,128,1024]{2,1,0:T(8,128)(2,1)}, u32[]{:S(2)}, u32[]{:S(2)}) collective-permute-start(bf16[8,128,1024]{2,1,0:T(8,128)(2,1)} %get-tuple-element.767), channel_id=1, source_target_pairs={{0,16},{8,24},{16,0},{24,8},{1,17},{9,25},{17,1},{25,9},{2,18},{10... | collective-permute-start | bytes 6291464 | tf_op jit(solution)/shard_map/ppermute | solution.py:614
  285.4 42.4 %all-to-all-start.5 = ((bf16[8,1,3,256,128]{4,3,2,1,0:T(8,128)(2,1)}), bf16[8,1,3,256,128]{4,3,2,1,0:T(8,128)(2,1)}, u32[]{:S(2)}, u32[]{:S(2)}) async-start(bf16[8,1,3,256,128]{4,3,2,1,0:T(8,128)(2,1)} %get-tuple-element.421), calls=%async_computation.5 | async-start | bytes 3145728 | tf_op jit(solution)/shard_map/cond/branch_1_fun/all_to_all | solution.py:42
  331.1 45.3 %collective-permute-start.27 = (bf16[4,128,1024]{2,1,0:T(8,128)(2,1)S(1)}, bf16[4,128,1024]{2,1,0:T(8,128)(2,1)}, u32[]{:S(2)}, u32[]{:S(2)}) collective-permute-start(bf16[4,128,1024]{2,1,0:T(8,128)(2,1)S(1)} %get-tuple-element.763), channel_id=1, source_target_pairs={{0,1},{1,0},{2,3},{3,2},{4,5},{5,4},{6,7},{7,6},{8,9},{9,8},{10,11... | collective-permute-start | bytes 3145736 | tf_op jit(solution)/shard_map/ppermute | solution.py:614
  333.9 42.3 %all-to-all-start.6 = ((bf16[8,1,3,256,128]{4,3,2,1,0:T(8,128)(2,1)}), bf16[8,1,3,256,128]{4,3,2,1,0:T(8,128)(2,1)}, u32[]{:S(2)}, u32[]{:S(2)}) async-start(bf16[8,1,3,256,128]{4,3,2,1,0:T(8,128)(2,1)} %get-tuple-element.450), calls=%async_computation.6 | async-start | bytes 3145728 | tf_op jit(solution)/shard_map/cond/branch_1_fun/all_to_all | solution.py:42
  380.4 42.4 %collective-permute-start.29 = (bf16[4,128,1024]{2,1,0:T(8,128)(2,1)}, bf16[4,128,1024]{2,1,0:T(8,128)(2,1)}, u32[]{:S(2)}, u32[]{:S(2)}) collective-permute-start(bf16[4,128,1024]{2,1,0:T(8,128)(2,1)} %get-tuple-element.774), channel_id=1, source_target_pairs={{0,1},{1,0},{2,3},{3,2},{4,5},{5,4},{6,7},{7,6},{8,9},{9,8},{10,11... | collective-permute-start | bytes 3145736 | tf_op jit(solution)/shard_map/ppermute | solution.py:614
  381.9 40.8 %collective-permute-start.28 = (bf16[2,128,1024]{2,1,0:T(8,128)(2,1)}, bf16[2,128,1024]{2,1,0:T(8,128)(2,1)}, u32[]{:S(2)}, u32[]{:S(2)}) collective-permute-start(bf16[2,128,1024]{2,1,0:T(8,128)(2,1)} %get-tuple-element.773), channel_id=1, source_target_pairs={{0,2},{1,3},{2,0},{3,1},{4,6},{5,7},{6,4},{7,5},{8,10},{9,11},{10,... | collective-permute-start | bytes 1572872 | tf_op jit(solution)/shard_map/ppermute | solution.py:614
  381.9 40.8 %all-to-all-start.3 = ((bf16[8,1,3,256,128]{4,3,2,1,0:T(8,128)(2,1)}), bf16[8,1,3,256,128]{4,3,2,1,0:T(8,128)(2,1)}, u32[]{:S(2)}, u32[]{:S(2)}) async-start(bf16[8,1,3,256,128]{4,3,2,1,0:T(8,128)(2,1)} %get-tuple-element.475), calls=%async_computation.3 | async-start | bytes 3145728 | tf_op jit(solution)/shard_map/cond/branch_1_fun/all_to_all | solution.py:42
  434.3 18.8 %collective-permute-start.32 = (bf16[8,128,512]{2,1,0:T(8,128)(2,1)}, bf16[8,128,512]{2,1,0:T(8,128)(2,1)}, u32[]{:S(2)}, u32[]{:S(2)}) collective-permute-start(bf16[8,128,512]{2,1,0:T(8,128)(2,1)} %weight_part.35), channel_id=1, source_target_pairs={{0,8},{8,0},{16,24},{24,16},{1,9},{9,1},{17,25},{25,17},{2,10},{10... | collective-permute-start | bytes 3145736 | tf_op jit(solution)/shard_map/ppermute | solution.py:614
  435.1 41.4 %collective-permute-start.35 = (bf16[4,128,512]{2,1,0:T(8,128)(2,1)}, bf16[4,128,512]{2,1,0:T(8,128)(2,1)}, u32[]{:S(2)}, u32[]{:S(2)}) collective-permute-start(bf16[4,128,512]{2,1,0:T(8,128)(2,1)} %get-tuple-element.809), channel_id=1, source_target_pairs={{0,1},{1,0},{2,3},{3,2},{4,5},{5,4},{6,7},{7,6},{8,9},{9,8},{10,11... | collective-permute-start | bytes 1572872 | tf_op jit(solution)/shard_map/ppermute | solution.py:614
  442.0 29.7 %collective-permute-start.31 = (bf16[8,128,512]{2,1,0:T(8,128)(2,1)}, bf16[8,128,512]{2,1,0:T(8,128)(2,1)S(1)}, u32[]{:S(2)}, u32[]{:S(2)}) collective-permute-start(bf16[8,128,512]{2,1,0:T(8,128)(2,1)} %weight_part.36), channel_id=1, source_target_pairs={{0,16},{8,24},{16,0},{24,8},{1,17},{9,25},{17,1},{25,9},{2,18},{10... | collective-permute-start | bytes 3145736 | tf_op jit(solution)/shard_map/ppermute | solution.py:614
  451.0 20.2 %collective-permute-start.34 = (bf16[2,128,1024]{2,1,0:T(8,128)(2,1)S(1)}, bf16[2,128,1024]{2,1,0:T(8,128)(2,1)S(1)}, u32[]{:S(2)}, u32[]{:S(2)}) collective-permute-start(bf16[2,128,1024]{2,1,0:T(8,128)(2,1)S(1)} %get-tuple-element.802), channel_id=1, source_target_pairs={{0,2},{1,3},{2,0},{3,1},{4,6},{5,7},{6,4},{7,5},{8,10},{9,11},{10,... | collective-permute-start | bytes 1572872 | tf_op jit(solution)/shard_map/ppermute | solution.py:614
  451.0 20.2 %collective-permute-start.33 = (bf16[1,128,1024]{2,1,0:T(8,128)(2,1)}, bf16[1,128,1024]{2,1,0:T(8,128)(2,1)S(1)}, u32[]{:S(2)}, u32[]{:S(2)}) collective-permute-start(bf16[1,128,1024]{2,1,0:T(8,128)(2,1)} %get-tuple-element.801), channel_id=1, source_target_pairs={{0,4},{1,5},{2,6},{3,7},{4,0},{5,1},{6,2},{7,3},{8,12},{9,13},{10,... | collective-permute-start | bytes 786440 | tf_op jit(solution)/shard_map/ppermute | solution.py:614
  479.7 17.9 %collective-permute-start.1 = (bf16[4,128,512]{2,1,0:T(8,128)(2,1)S(1)}, bf16[4,128,512]{2,1,0:T(8,128)(2,1)}, u32[]{:S(2)}, u32[]{:S(2)}) collective-permute-start(bf16[4,128,512]{2,1,0:T(8,128)(2,1)S(1)} %get-tuple-element.519), channel_id=1, source_target_pairs={{0,1},{1,0},{2,3},{3,2},{4,5},{5,4},{6,7},{7,6},{8,9},{9,8},{10,11... | collective-permute-start | bytes 1572872 | tf_op jit(solution)/shard_map/cond/branch_1_fun/ppermute | solution.py:614
  480.7 18.2 %collective-permute-start.2 = (bf16[2,128,1024]{2,1,0:T(8,128)(2,1)S(1)}, bf16[2,128,1024]{2,1,0:T(8,128)(2,1)}, u32[]{:S(2)}, u32[]{:S(2)}) collective-permute-start(bf16[2,128,1024]{2,1,0:T(8,128)(2,1)S(1)} %get-tuple-element.520), channel_id=1, source_target_pairs={{0,2},{1,3},{2,0},{3,1},{4,6},{5,7},{6,4},{7,5},{8,10},{9,11},{10,... | collective-permute-start | bytes 1572872 | tf_op jit(solution)/shard_map/cond/branch_1_fun/ppermute | solution.py:614
  (69 other events, 581.8 us)
